TPU v7x, 512 devices: a whole 4x4x16 slice. The times are simulated.
512 devices in a mesh: dp: 32 (over x, z_lo, core), ctx: 16 (over z_hi, y).
Axes of the slice: x: 4, y: 4, z: 16 (z_hi: 4, z_lo: 4; z = z_hi * 4 + z_lo), core: 2. Of those that a mesh axis runs over, the one named last changes fastest.
Arguments:
- grad_out: bfloat16 [16384, 8192], P('ctx', 'dp'), may hold values from -6 to 6
- conv_input: bfloat16 [16384, 8192], P('ctx', 'dp'), may hold values from -6 to 6
- residues: float32 [256, 8], replicated, may hold values from -0.12 to 0.12
- log_rate: float32 [256, 8], replicated, as said below
Outputs:
- grad_input: bfloat16 [16384, 8192], P('ctx', 'dp')
- grad_residue: float32 [256, 8], P('ctx')
- grad_lograte: float32 [256, 8], P('ctx')
Inputs may be any that keep to these rules, and one draw needn't show every extreme that they name: The rates exp(log_rate) lie between 0.1 / 16384 and 1 / 16.
All inputs are finite; a program needn't handle non-finite values.
Results may differ from a plain program's by a relative error of at most 0.014.
Values may be sent and summed in bfloat16 or wider, within the bound.
No kernel may reach another device: no remote copies, remote signals or barrier semaphores. Data moves between devices by JAX's collectives and lax.ppermute only.
A program may use at most 64 MiB of HBM per device.

v0:
```python
import jax
import jax.numpy as jnp
from jax import lax
from jax.sharding import PartitionSpec as P


def state_combine(rate, earlier, later):
    decay = jnp.exp(-rate * later[2])
    w_new = decay * earlier[0] + later[0]
    q_new = decay * (earlier[1] + later[2] * earlier[0]) + later[1]
    return (w_new, q_new, earlier[2] + later[2])


def block_pass(upstream, inputs, rate, resid, blk):
    count, width = upstream.shape
    blocks = count // blk
    pos = jnp.arange(blk, dtype=jnp.float32)
    up_blocks = upstream.reshape(blocks, blk, width)
    in_blocks = inputs.reshape(blocks, blk, width)
    lowered = jnp.exp(-rate[None] * pos[:, None, None])
    raised = jnp.exp(rate[None] * pos[:, None, None])
    tail = jnp.exp(-rate[None] * (blk - pos)[:, None, None])
    first = up_blocks[..., None] * lowered[None]
    second = first * pos[None, :, None, None]
    upper = (pos[:, None] <= pos[None, :]).astype(jnp.float32)
    summed = jnp.einsum(
        "st,jktcm->jkscm", upper, jnp.stack([first, second]), precision=lax.Precision.HIGHEST
    )
    w_local = raised[None] * summed[0]
    q_local = raised[None] * (summed[1] - pos[None, :, None, None] * summed[0])
    spans = jnp.full((blocks, 1, 1), float(blk), jnp.float32)
    flipped = (w_local[::-1, 0], q_local[::-1, 0], spans)
    inclusive = lax.associative_scan(lambda left, right: state_combine(rate, left, right), flipped)
    w_incl = inclusive[0][::-1]
    q_incl = inclusive[1][::-1]
    w_begin = w_incl[0]
    q_begin = q_incl[0]
    zeros = jnp.zeros_like(w_incl[:1])
    w_in = jnp.concatenate([w_incl[1:], zeros], axis=0)
    q_in = jnp.concatenate([q_incl[1:], zeros], axis=0)
    w_full = w_local + tail[None] * w_in[:, None]
    q_full = q_local + tail[None] * (
        q_in[:, None] + (blk - pos)[None, :, None, None] * w_in[:, None]
    )
    grad_in = jnp.einsum("kscm,cm->ksc", w_full, resid).reshape(count, width)
    res_sum = jnp.sum(in_blocks[..., None] * w_full, axis=(0, 1))
    lag_sum = jnp.sum(in_blocks[..., None] * q_full, axis=(0, 1))
    behind = blocks - 1 - jnp.arange(blocks, dtype=jnp.float32)
    distant = jnp.exp(-rate[None] * blk * behind[:, None, None])
    near_in = jnp.sum(in_blocks[..., None] * tail[None], axis=1)
    far_in = jnp.sum(in_blocks[..., None] * ((blk - pos)[:, None, None] * tail)[None], axis=1)
    near = jnp.sum(distant * near_in, axis=0)
    far = jnp.sum(distant * (far_in + blk * behind[:, None, None] * near_in), axis=0)
    return (grad_in, res_sum, lag_sum, w_begin, q_begin, near, far)


def slab_pass(upstream, inputs, rate, resid, blk):
    count, width = upstream.shape
    pieces = 8
    slab = width // pieces

    def split_rows(array):
        return array.reshape(count, pieces, slab).transpose(1, 0, 2)

    def split_modes(array):
        return array.reshape(pieces, slab, array.shape[1])

    results = lax.map(
        lambda item: block_pass(item[0], item[1], item[2], item[3], blk),
        (split_rows(upstream), split_rows(inputs), split_modes(rate), split_modes(resid)),
    )
    grad_in = results[0].transpose(1, 0, 2).reshape(count, width)
    rest = [piece.reshape(width, -1) for piece in results[1:]]
    return (grad_in,) + tuple(rest)


def on_device(grad_out, conv_input, residues, log_rate):
    n_context = lax.axis_size("ctx")
    tokens, chans = grad_out.shape
    filters, modes = residues.shape
    seqlen = tokens * n_context
    blk = min(64, tokens)
    rate = jnp.exp(log_rate)
    narrow = chans // n_context
    shaped = (tokens, n_context, narrow)
    up_cols, in_cols = (
        lax.all_to_all(grad_out.reshape(shaped), "ctx", split_axis=1, concat_axis=0, tiled=True),
        lax.all_to_all(conv_input.reshape(shaped), "ctx", split_axis=1, concat_axis=0, tiled=True),
    )
    up_cols = up_cols.reshape(seqlen, narrow).astype(jnp.float32)
    in_cols = in_cols.reshape(seqlen, narrow).astype(jnp.float32)
    channel_ids = (
        lax.axis_index("dp") * chans
        + lax.axis_index("ctx") * narrow
        + jnp.arange(narrow, dtype=jnp.int32)
    )
    owner = ((channel_ids % filters)[:, None] == jnp.arange(filters, dtype=jnp.int32)[None]).astype(
        jnp.float32
    )
    rate_cols = jnp.dot(owner, rate, precision=lax.Precision.HIGHEST)
    resid_cols = jnp.dot(owner, residues, precision=lax.Precision.HIGHEST)
    grad_in, res_sum, lag_sum, w_begin, q_begin, near, far = slab_pass(
        up_cols, in_cols, rate_cols, resid_cols, blk
    )
    returned = lax.all_to_all(
        grad_in.astype(jnp.bfloat16).reshape(seqlen, 1, narrow),
        "ctx",
        split_axis=0,
        concat_axis=1,
        tiled=True,
    )
    grad_input = returned.reshape(tokens, chans)
    res_term = res_sum / seqlen
    lag_term = -rate_cols * resid_cols * lag_sum / seqlen
    partial_value = (
        jnp.dot(owner.T, res_term, precision=lax.Precision.HIGHEST),
        jnp.dot(owner.T, lag_term, precision=lax.Precision.HIGHEST),
    )
    shares = (
        lax.psum_scatter(partial_value[0], "ctx", scatter_dimension=0, tiled=True),
        lax.psum_scatter(partial_value[1], "ctx", scatter_dimension=0, tiled=True),
    )
    grad_residue, grad_lograte = lax.psum((shares[0], shares[1]), "dp")
    return (grad_input, grad_residue, grad_lograte)


def solution(mesh):
    in_specs = (P("ctx", "dp"), P("ctx", "dp"), P(), P())
    out_specs = (P("ctx", "dp"), P("ctx", None), P("ctx", None))
    return jax.shard_map(
        on_device, mesh=mesh, in_specs=in_specs, out_specs=out_specs, check_vma=False
    )
```

profile of v0, /device:TPU:1, one launch (start us, length us, event | category | flops | bytes accessed | tf_op | source)
XLA Modules:
  0.0 698.1 jit_solution(3427567044258233443)
XLA Ops:
  7.2 2.1 copy.97
  9.3 18.4 %all-to-all-start = ((bf16[1024,16,16]{0,2,1:T(8,128)(2,1)}), bf16[1024,16,16]{0,2,1:T(8,128)(2,1)S(1)}, u32[]{:S(2)}, u32[]{:S(2)}) async-start(bf16[1024,16,16]{0,2,1:T(8,128)(2,1)} %bitcast.17), calls=%async_computation | async-start | bytes 1048576 | tf_op jit(solution)/shard_map/all_to_all | solution.py:87
  27.7 1.0 copy.99
  28.7 18.5 %all-to-all-done = bf16[1024,16,16]{0,2,1:T(8,128)(2,1)S(1)} async-done(((bf16[1024,16,16]{0,2,1:T(8,128)(2,1)}), bf16[1024,16,16]{0,2,1:T(8,128)(2,1)S(1)}, u32[]{:S(2)}, u32[]{:S(2)}) %all-to-all-start) | async-done | bytes 524320 | tf_op jit(solution)/shard_map/all_to_all | solution.py:87
  47.2 16.8 %all-to-all-start.1 = ((bf16[1024,16,16]{0,2,1:T(8,128)(2,1)}), bf16[1024,16,16]{0,2,1:T(8,128)(2,1)S(1)}, u32[]{:S(2)}, u32[]{:S(2)}) async-start(bf16[1024,16,16]{0,2,1:T(8,128)(2,1)} %bitcast.21), calls=%async_computation.1 | async-start | bytes 1048576 | tf_op jit(solution)/shard_map/all_to_all | solution.py:88
  66.6 0.9 reshape.122
  67.5 14.0 %all-to-all-done.1 = bf16[1024,16,16]{0,2,1:T(8,128)(2,1)S(1)} async-done(((bf16[1024,16,16]{0,2,1:T(8,128)(2,1)}), bf16[1024,16,16]{0,2,1:T(8,128)(2,1)S(1)}, u32[]{:S(2)}, u32[]{:S(2)}) %all-to-all-start.1) | async-done | bytes 524320 | tf_op jit(solution)/shard_map/all_to_all | solution.py:88
  82.2 1.9 reshape.123
  84.1 249.5 %while.14 = (s32[]{:T(128)}, bf16[8,16384,2]{1,2,0:T(2,128)(2,1)}, f32[8,2,8]{2,1,0:T(2,128)}, f32[8,2,8]{2,1,0:T(2,128)}, f32[8,2,8]{2,1,0:T(2,128)}, /*index=5...) while((s32[]{:T(128)}, bf16[8,16384,2]{1,2,0:T(2,128)(2,1)}, ...), condition=%wide.region_3.4_spmd, body=%wide.region_0.3_spmd.sunk | while | flops 408246176 | bytes 17257028 | solution.py:68
  84.1 1.2 constant_dynamic-slice_fusion.8
  87.6 0.9 constant_dynamic-slice_fusion.11
  89.4 1.2 fusion.60
  102.0 0.8 multiply_add_fusion.43
  112.0 1.2 multiply_reduce_fusion.3
  115.3 1.2 constant_dynamic-slice_fusion.8
  118.7 0.9 constant_dynamic-slice_fusion.11
  120.5 1.2 fusion.60
  133.2 0.8 multiply_add_fusion.43
  143.2 1.2 multiply_reduce_fusion.3
  146.4 1.2 constant_dynamic-slice_fusion.8
  149.9 0.9 constant_dynamic-slice_fusion.11
  151.7 1.2 fusion.60
  164.4 0.8 multiply_add_fusion.43
  174.3 1.2 multiply_reduce_fusion.3
  177.6 1.3 constant_dynamic-slice_fusion.8
  181.1 0.9 constant_dynamic-slice_fusion.11
  183.0 1.2 fusion.60
  195.6 0.8 multiply_add_fusion.43
  205.6 1.2 multiply_reduce_fusion.3
  208.8 1.2 constant_dynamic-slice_fusion.8
  212.3 0.9 constant_dynamic-slice_fusion.11
  214.2 1.2 fusion.60
  226.8 0.8 multiply_add_fusion.43
  236.8 1.2 multiply_reduce_fusion.3
  240.0 1.2 constant_dynamic-slice_fusion.8
  243.5 0.9 constant_dynamic-slice_fusion.11
  245.3 1.2 fusion.60
  258.0 0.8 multiply_add_fusion.43
  267.9 1.2 multiply_reduce_fusion.3
  271.2 1.2 constant_dynamic-slice_fusion.8
  274.6 0.9 constant_dynamic-slice_fusion.11
  276.4 1.2 fusion.60
  289.1 0.8 multiply_add_fusion.43
  299.1 1.2 multiply_reduce_fusion.3
  302.3 1.2 constant_dynamic-slice_fusion.8
  305.8 0.9 constant_dynamic-slice_fusion.11
  307.7 1.2 fusion.60
  320.3 0.8 multiply_add_fusion.43
  330.3 1.2 multiply_reduce_fusion.3
  333.5 1.2 convert_element_type.48
  335.3 1.0 reduce.3
  336.3 3.1 copy.124
  339.4 6.5 reshape.136
  345.9 8.3 %all-to-all-start.2 = ((bf16[16,2,8192]{2,1,0:T(2,128)(2,1)}), bf16[16,2,8192]{2,1,0:T(2,128)(2,1)S(1)}, u32[]{:S(2)}, u32[]{:S(2)}) async-start(bf16[16,2,8192]{2,1,0:T(2,128)(2,1)} %reshape.136), calls=%async_computation.2 | async-start | bytes 1048576 | tf_op jit(solution)/shard_map/all_to_all | solution.py:105
  354.3 1.0 fusion.28
  355.5 1.0 fusion.29
  356.5 126.3 %reduce-scatter.9.cloned.1.call-done = f32[16,8]{1,0:T(8,128)} async-done(((f32[256,8]{1,0:T(8,128)}), f32[16,8]{1,0:T(8,128)}) %reduce-scatter.9.cloned.1.call-update) | async-done | bytes 528
  482.8 0.8 copy.114
  483.6 109.7 %reduce-scatter.7.cloned.1.call-done = f32[16,8]{1,0:T(8,128)} async-done(((f32[256,8]{1,0:T(8,128)}), f32[16,8]{1,0:T(8,128)}) %reduce-scatter.7.cloned.1.call-update) | async-done | bytes 528
  593.3 0.8 copy.112
  594.0 70.9 %all-reduce.34 = (f32[16,8]{0,1:T(8,128)}, f32[16,8]{0,1:T(8,128)}) all-reduce(f32[16,8]{0,1:T(8,128)S(1)} %copy.112, f32[16,8]{0,1:T(8,128)S(1)} %copy.114), channel_id=1, replica_groups=mesh['dp'=32,'ctx'=16] {'dp'}, use_global_device_ids=true, to_apply=%region_5.6 | all-reduce | flops 256 | bytes 2048 | tf_op jit(solution)/shard_map/psum | solution.py:123
  664.9 9.8 %reshape.137 = bf16[16384,1,16]{2,1,0:T(2,128)(2,1)} reshape(bf16[16,2,8192]{2,1,0:T(2,128)(2,1)S(1)} %all-to-all-done.2) | data formatting | bytes 1048576
  674.8 14.9 %copy.103 = bf16[16384,1,16]{0,2,1:T(8,128)(2,1)S(1)} copy(bf16[16384,1,16]{2,1,0:T(2,128)(2,1)} %reshape.137) | data formatting | bytes 1048576 | tf_op jit(solution)/shard_map/all_to_all | solution.py:105
  690.3 1.0 copy.106
  (1324 shorter events, 207.8 us)
Async XLA Ops:
  7.2 57.8 %copy-start = (f32[256,8]{0,1:T(8,128)S(1)}, f32[256,8]{0,1:T(8,128)}, u32[]{:S(2)}) copy-start(f32[256,8]{0,1:T(8,128)} %param.8) | copy-start | bytes 24580
  7.2 20.5 %copy-start.1 = (bf16[1024,256]{1,0:T(8,128)(2,1)S(1)}, bf16[1024,256]{1,0:T(8,128)(2,1)}, u32[]{:S(2)}) copy-start(bf16[1024,256]{1,0:T(8,128)(2,1)} %param.7) | copy-start | bytes 1572868
  7.2 56.9 %copy-start.17 = (f32[256,8]{0,1:T(8,128)S(1)}, f32[256,8]{0,1:T(8,128)}, u32[]{:S(2)}) copy-start(f32[256,8]{0,1:T(8,128)} %param.9) | copy-start | bytes 24580
  9.3 37.9 %all-to-all-start = ((bf16[1024,16,16]{0,2,1:T(8,128)(2,1)}), bf16[1024,16,16]{0,2,1:T(8,128)(2,1)S(1)}, u32[]{:S(2)}, u32[]{:S(2)}) async-start(bf16[1024,16,16]{0,2,1:T(8,128)(2,1)} %bitcast.17), calls=%async_computation | async-start | bytes 1048576 | tf_op jit(solution)/shard_map/all_to_all | solution.py:87
  47.2 34.3 %all-to-all-start.1 = ((bf16[1024,16,16]{0,2,1:T(8,128)(2,1)}), bf16[1024,16,16]{0,2,1:T(8,128)(2,1)S(1)}, u32[]{:S(2)}, u32[]{:S(2)}) async-start(bf16[1024,16,16]{0,2,1:T(8,128)(2,1)} %bitcast.21), calls=%async_computation.1 | async-start | bytes 1048576 | tf_op jit(solution)/shard_map/all_to_all | solution.py:88
  87.5 5.8 copy-start.2
  87.5 7.4 %copy-start.3 = (f32[2,8]{1,0:T(2,128)}, f32[2,8]{1,0:T(2,128)S(1)}, u32[]{:S(2)}) copy-start(f32[2,8]{1,0:T(2,128)S(1)} %get-tuple-element.294) | copy-start | bytes 196 | tf_op jit(solution)/shard_map/while
  87.5 8.4 %copy-start.4 = (f32[2,8]{1,0:T(2,128)}, f32[2,8]{1,0:T(2,128)S(1)}, u32[]{:S(2)}) copy-start(f32[2,8]{1,0:T(2,128)S(1)} %get-tuple-element.297) | copy-start | bytes 196 | tf_op jit(solution)/shard_map/while
  87.5 9.1 %copy-start.5 = (f32[2,8]{1,0:T(2,128)}, f32[2,8]{1,0:T(2,128)S(1)}, u32[]{:S(2)}) copy-start(f32[2,8]{1,0:T(2,128)S(1)} %get-tuple-element.300) | copy-start | bytes 196 | tf_op jit(solution)/shard_map/while
  87.5 9.7 %copy-start.6 = (f32[2,8]{1,0:T(2,128)}, f32[2,8]{1,0:T(2,128)S(1)}, u32[]{:S(2)}) copy-start(f32[2,8]{1,0:T(2,128)S(1)} %get-tuple-element.303) | copy-start | bytes 196 | tf_op jit(solution)/shard_map/while
  102.8 10.4 %copy-start.7 = (f32[1,2,8]{2,1,0:T(2,128)S(1)}, f32[1,2,8]{2,1,0:T(2,128)}, u32[]{:S(2)}) copy-start(f32[1,2,8]{2,1,0:T(2,128)} %constant_dynamic-slice_fusion.8) | copy-start | bytes 196 | tf_op jit(solution)/shard_map/while
  118.6 5.8 copy-start.2
  118.6 7.4 %copy-start.3 = (f32[2,8]{1,0:T(2,128)}, f32[2,8]{1,0:T(2,128)S(1)}, u32[]{:S(2)}) copy-start(f32[2,8]{1,0:T(2,128)S(1)} %get-tuple-element.294) | copy-start | bytes 196 | tf_op jit(solution)/shard_map/while
  118.6 8.4 %copy-start.4 = (f32[2,8]{1,0:T(2,128)}, f32[2,8]{1,0:T(2,128)S(1)}, u32[]{:S(2)}) copy-start(f32[2,8]{1,0:T(2,128)S(1)} %get-tuple-element.297) | copy-start | bytes 196 | tf_op jit(solution)/shard_map/while
  118.6 9.1 %copy-start.5 = (f32[2,8]{1,0:T(2,128)}, f32[2,8]{1,0:T(2,128)S(1)}, u32[]{:S(2)}) copy-start(f32[2,8]{1,0:T(2,128)S(1)} %get-tuple-element.300) | copy-start | bytes 196 | tf_op jit(solution)/shard_map/while
  118.6 9.7 %copy-start.6 = (f32[2,8]{1,0:T(2,128)}, f32[2,8]{1,0:T(2,128)S(1)}, u32[]{:S(2)}) copy-start(f32[2,8]{1,0:T(2,128)S(1)} %get-tuple-element.303) | copy-start | bytes 196 | tf_op jit(solution)/shard_map/while
  133.9 10.4 %copy-start.7 = (f32[1,2,8]{2,1,0:T(2,128)S(1)}, f32[1,2,8]{2,1,0:T(2,128)}, u32[]{:S(2)}) copy-start(f32[1,2,8]{2,1,0:T(2,128)} %constant_dynamic-slice_fusion.8) | copy-start | bytes 196 | tf_op jit(solution)/shard_map/while
  149.8 5.8 copy-start.2
  149.8 7.4 %copy-start.3 = (f32[2,8]{1,0:T(2,128)}, f32[2,8]{1,0:T(2,128)S(1)}, u32[]{:S(2)}) copy-start(f32[2,8]{1,0:T(2,128)S(1)} %get-tuple-element.294) | copy-start | bytes 196 | tf_op jit(solution)/shard_map/while
  149.8 8.4 %copy-start.4 = (f32[2,8]{1,0:T(2,128)}, f32[2,8]{1,0:T(2,128)S(1)}, u32[]{:S(2)}) copy-start(f32[2,8]{1,0:T(2,128)S(1)} %get-tuple-element.297) | copy-start | bytes 196 | tf_op jit(solution)/shard_map/while
  149.8 9.1 %copy-start.5 = (f32[2,8]{1,0:T(2,128)}, f32[2,8]{1,0:T(2,128)S(1)}, u32[]{:S(2)}) copy-start(f32[2,8]{1,0:T(2,128)S(1)} %get-tuple-element.300) | copy-start | bytes 196 | tf_op jit(solution)/shard_map/while
  149.8 9.7 %copy-start.6 = (f32[2,8]{1,0:T(2,128)}, f32[2,8]{1,0:T(2,128)S(1)}, u32[]{:S(2)}) copy-start(f32[2,8]{1,0:T(2,128)S(1)} %get-tuple-element.303) | copy-start | bytes 196 | tf_op jit(solution)/shard_map/while
  165.1 10.4 %copy-start.7 = (f32[1,2,8]{2,1,0:T(2,128)S(1)}, f32[1,2,8]{2,1,0:T(2,128)}, u32[]{:S(2)}) copy-start(f32[1,2,8]{2,1,0:T(2,128)} %constant_dynamic-slice_fusion.8) | copy-start | bytes 196 | tf_op jit(solution)/shard_map/while
  177.6 5.4 copy-start.8
  181.0 5.8 copy-start.2
  181.0 7.4 %copy-start.3 = (f32[2,8]{1,0:T(2,128)}, f32[2,8]{1,0:T(2,128)S(1)}, u32[]{:S(2)}) copy-start(f32[2,8]{1,0:T(2,128)S(1)} %get-tuple-element.294) | copy-start | bytes 196 | tf_op jit(solution)/shard_map/while
  181.0 8.4 %copy-start.4 = (f32[2,8]{1,0:T(2,128)}, f32[2,8]{1,0:T(2,128)S(1)}, u32[]{:S(2)}) copy-start(f32[2,8]{1,0:T(2,128)S(1)} %get-tuple-element.297) | copy-start | bytes 196 | tf_op jit(solution)/shard_map/while
  181.0 9.1 %copy-start.5 = (f32[2,8]{1,0:T(2,128)}, f32[2,8]{1,0:T(2,128)S(1)}, u32[]{:S(2)}) copy-start(f32[2,8]{1,0:T(2,128)S(1)} %get-tuple-element.300) | copy-start | bytes 196 | tf_op jit(solution)/shard_map/while
  181.0 9.7 %copy-start.6 = (f32[2,8]{1,0:T(2,128)}, f32[2,8]{1,0:T(2,128)S(1)}, u32[]{:S(2)}) copy-start(f32[2,8]{1,0:T(2,128)S(1)} %get-tuple-element.303) | copy-start | bytes 196 | tf_op jit(solution)/shard_map/while
  196.4 10.4 %copy-start.7 = (f32[1,2,8]{2,1,0:T(2,128)S(1)}, f32[1,2,8]{2,1,0:T(2,128)}, u32[]{:S(2)}) copy-start(f32[1,2,8]{2,1,0:T(2,128)} %constant_dynamic-slice_fusion.8) | copy-start | bytes 196 | tf_op jit(solution)/shard_map/while
  208.8 5.3 copy-start.8
  212.2 5.8 copy-start.2
  212.3 7.4 %copy-start.3 = (f32[2,8]{1,0:T(2,128)}, f32[2,8]{1,0:T(2,128)S(1)}, u32[]{:S(2)}) copy-start(f32[2,8]{1,0:T(2,128)S(1)} %get-tuple-element.294) | copy-start | bytes 196 | tf_op jit(solution)/shard_map/while
  212.3 8.4 %copy-start.4 = (f32[2,8]{1,0:T(2,128)}, f32[2,8]{1,0:T(2,128)S(1)}, u32[]{:S(2)}) copy-start(f32[2,8]{1,0:T(2,128)S(1)} %get-tuple-element.297) | copy-start | bytes 196 | tf_op jit(solution)/shard_map/while
  212.3 9.1 %copy-start.5 = (f32[2,8]{1,0:T(2,128)}, f32[2,8]{1,0:T(2,128)S(1)}, u32[]{:S(2)}) copy-start(f32[2,8]{1,0:T(2,128)S(1)} %get-tuple-element.300) | copy-start | bytes 196 | tf_op jit(solution)/shard_map/while
  212.3 9.7 %copy-start.6 = (f32[2,8]{1,0:T(2,128)}, f32[2,8]{1,0:T(2,128)S(1)}, u32[]{:S(2)}) copy-start(f32[2,8]{1,0:T(2,128)S(1)} %get-tuple-element.303) | copy-start | bytes 196 | tf_op jit(solution)/shard_map/while
  227.6 10.4 %copy-start.7 = (f32[1,2,8]{2,1,0:T(2,128)S(1)}, f32[1,2,8]{2,1,0:T(2,128)}, u32[]{:S(2)}) copy-start(f32[1,2,8]{2,1,0:T(2,128)} %constant_dynamic-slice_fusion.8) | copy-start | bytes 196 | tf_op jit(solution)/shard_map/while
  243.4 5.8 copy-start.2
  243.4 7.4 %copy-start.3 = (f32[2,8]{1,0:T(2,128)}, f32[2,8]{1,0:T(2,128)S(1)}, u32[]{:S(2)}) copy-start(f32[2,8]{1,0:T(2,128)S(1)} %get-tuple-element.294) | copy-start | bytes 196 | tf_op jit(solution)/shard_map/while
  243.4 8.4 %copy-start.4 = (f32[2,8]{1,0:T(2,128)}, f32[2,8]{1,0:T(2,128)S(1)}, u32[]{:S(2)}) copy-start(f32[2,8]{1,0:T(2,128)S(1)} %get-tuple-element.297) | copy-start | bytes 196 | tf_op jit(solution)/shard_map/while
  243.4 9.1 %copy-start.5 = (f32[2,8]{1,0:T(2,128)}, f32[2,8]{1,0:T(2,128)S(1)}, u32[]{:S(2)}) copy-start(f32[2,8]{1,0:T(2,128)S(1)} %get-tuple-element.300) | copy-start | bytes 196 | tf_op jit(solution)/shard_map/while
  243.4 9.7 %copy-start.6 = (f32[2,8]{1,0:T(2,128)}, f32[2,8]{1,0:T(2,128)S(1)}, u32[]{:S(2)}) copy-start(f32[2,8]{1,0:T(2,128)S(1)} %get-tuple-element.303) | copy-start | bytes 196 | tf_op jit(solution)/shard_map/while
  258.7 10.4 %copy-start.7 = (f32[1,2,8]{2,1,0:T(2,128)S(1)}, f32[1,2,8]{2,1,0:T(2,128)}, u32[]{:S(2)}) copy-start(f32[1,2,8]{2,1,0:T(2,128)} %constant_dynamic-slice_fusion.8) | copy-start | bytes 196 | tf_op jit(solution)/shard_map/while
  274.5 5.8 copy-start.2
  274.5 7.4 %copy-start.3 = (f32[2,8]{1,0:T(2,128)}, f32[2,8]{1,0:T(2,128)S(1)}, u32[]{:S(2)}) copy-start(f32[2,8]{1,0:T(2,128)S(1)} %get-tuple-element.294) | copy-start | bytes 196 | tf_op jit(solution)/shard_map/while
  274.5 8.4 %copy-start.4 = (f32[2,8]{1,0:T(2,128)}, f32[2,8]{1,0:T(2,128)S(1)}, u32[]{:S(2)}) copy-start(f32[2,8]{1,0:T(2,128)S(1)} %get-tuple-element.297) | copy-start | bytes 196 | tf_op jit(solution)/shard_map/while
  274.5 9.1 %copy-start.5 = (f32[2,8]{1,0:T(2,128)}, f32[2,8]{1,0:T(2,128)S(1)}, u32[]{:S(2)}) copy-start(f32[2,8]{1,0:T(2,128)S(1)} %get-tuple-element.300) | copy-start | bytes 196 | tf_op jit(solution)/shard_map/while
  274.5 9.7 %copy-start.6 = (f32[2,8]{1,0:T(2,128)}, f32[2,8]{1,0:T(2,128)S(1)}, u32[]{:S(2)}) copy-start(f32[2,8]{1,0:T(2,128)S(1)} %get-tuple-element.303) | copy-start | bytes 196 | tf_op jit(solution)/shard_map/while
  289.8 10.4 %copy-start.7 = (f32[1,2,8]{2,1,0:T(2,128)S(1)}, f32[1,2,8]{2,1,0:T(2,128)}, u32[]{:S(2)}) copy-start(f32[1,2,8]{2,1,0:T(2,128)} %constant_dynamic-slice_fusion.8) | copy-start | bytes 196 | tf_op jit(solution)/shard_map/while
  302.3 5.4 copy-start.8
  305.7 5.8 copy-start.2
  305.7 7.4 %copy-start.3 = (f32[2,8]{1,0:T(2,128)}, f32[2,8]{1,0:T(2,128)S(1)}, u32[]{:S(2)}) copy-start(f32[2,8]{1,0:T(2,128)S(1)} %get-tuple-element.294) | copy-start | bytes 196 | tf_op jit(solution)/shard_map/while
  305.7 8.4 %copy-start.4 = (f32[2,8]{1,0:T(2,128)}, f32[2,8]{1,0:T(2,128)S(1)}, u32[]{:S(2)}) copy-start(f32[2,8]{1,0:T(2,128)S(1)} %get-tuple-element.297) | copy-start | bytes 196 | tf_op jit(solution)/shard_map/while
  305.7 9.1 %copy-start.5 = (f32[2,8]{1,0:T(2,128)}, f32[2,8]{1,0:T(2,128)S(1)}, u32[]{:S(2)}) copy-start(f32[2,8]{1,0:T(2,128)S(1)} %get-tuple-element.300) | copy-start | bytes 196 | tf_op jit(solution)/shard_map/while
  305.8 9.7 %copy-start.6 = (f32[2,8]{1,0:T(2,128)}, f32[2,8]{1,0:T(2,128)S(1)}, u32[]{:S(2)}) copy-start(f32[2,8]{1,0:T(2,128)S(1)} %get-tuple-element.303) | copy-start | bytes 196 | tf_op jit(solution)/shard_map/while
  321.1 10.4 %copy-start.7 = (f32[1,2,8]{2,1,0:T(2,128)S(1)}, f32[1,2,8]{2,1,0:T(2,128)}, u32[]{:S(2)}) copy-start(f32[1,2,8]{2,1,0:T(2,128)} %constant_dynamic-slice_fusion.8) | copy-start | bytes 196 | tf_op jit(solution)/shard_map/while
  339.4 14.9 %copy-start.13 = (f32[8,2,8]{2,1,0:T(2,128)S(1)}, f32[8,2,8]{2,1,0:T(2,128)}, u32[]{:S(2)}) copy-start(f32[8,2,8]{2,1,0:T(2,128)} %get-tuple-element.49) | copy-start | bytes 1540
  339.4 15.0 %copy-start.10 = (f32[16,8]{0,1:T(8,128)S(1)}, f32[16,8]{0,1:T(8,128)}, u32[]{:S(2)}) copy-start(f32[16,8]{0,1:T(8,128)} %copy-done.9) | copy-start | bytes 1540
  339.4 15.0 %copy-start.12 = (f32[16,8]{0,1:T(8,128)S(1)}, f32[16,8]{0,1:T(8,128)}, u32[]{:S(2)}) copy-start(f32[16,8]{0,1:T(8,128)} %copy-done.11) | copy-start | bytes 1540
  339.4 15.0 %copy-start.16 = (s32[16]{0:T(128)S(1)}, s32[16]{0:T(128)}, u32[]{:S(2)}) copy-start(s32[16]{0:T(128)} %copy-done.15) | copy-start | bytes 196
  339.4 16.1 %copy-start.14 = (f32[8,2,8]{2,1,0:T(2,128)S(1)}, f32[8,2,8]{2,1,0:T(2,128)}, u32[]{:S(2)}) copy-start(f32[8,2,8]{2,1,0:T(2,128)} %get-tuple-element.48) | copy-start | bytes 1540
  345.9 319.1 %all-to-all-start.2 = ((bf16[16,2,8192]{2,1,0:T(2,128)(2,1)}), bf16[16,2,8192]{2,1,0:T(2,128)(2,1)S(1)}, u32[]{:S(2)}, u32[]{:S(2)}) async-start(bf16[16,2,8192]{2,1,0:T(2,128)(2,1)} %reshape.136), calls=%async_computation.2 | async-start | bytes 1048576 | tf_op jit(solution)/shard_map/all_to_all | solution.py:105
  354.2 128.6 %reduce-scatter.9.cloned.1.call-start = ((), (), s32[]{:S(2)}) async-start(), calls=%async_computation.6 | async-start | bytes 139264
  355.4 237.9 %reduce-scatter.7.cloned.1.call-start = ((), (), s32[]{:S(2)}) async-start(), calls=%async_computation.5 | async-start | bytes 139264
  (8 other events, 30.4 us)
Sparse Core Ops, SparseCore 0:
  359.1 123.6 reduce-scatter.8
  487.4 105.8 reduce-scatter.6
where the time goes:
time: 701 us; the launch traced here: 698 us
  waiting for transfers between devices  268 us (38%)
  local copies, waits for them, and re-layouts  198 us (28%)
  other arithmetic  84.1 us (12%)
  blocking collectives  70.9 us (10%)
  starting transfers between devices  43.6 us (6%)
  matrix products  15.3 us (2%)
  between operations  14.3 us (2%)
    unnamed x4, waiting for transfers between devices  236 us
    psum x1, blocking collectives, on_device(): grad_residue, grad_lograte = lax.psum((shares[0], shares[1]), 'dp')  70.9 us
    add x120, other arithmetic, state_combine(): w_new = decay * earlier[0] + later[0]  52.4 us
    slice x336, local copies, waits for them, and re-layouts, block_pass(): lax.associative_scan(lambda left, right: state_combine(rate, left, right)...  48.8 us
    pad x192, local copies, waits for them, and re-layouts, block_pass(): lax.associative_scan(lambda left, right: state_combine(rate, left, right)...  34.2 us
    dynamic_slice x48, local copies, waits for them, and re-layouts, slab_pass(): lax.map(lambda item: block_pass(item[0], item[1], item[2], item[3], blk),...  28.5 us
    unnamed x31, local copies, waits for them, and re-layouts  25.3 us
    all_to_all x1, waiting for transfers between devices, on_device(): lax.all_to_all(grad_out.reshape(shaped), 'ctx', split_axis=1, concat_axis...  18.5 us
  transfers between devices with their start and end apart: 5, of which 4 were waited for; matrix products, arithmetic and copies ran while one was open for 1% of the time, Pallas kernels for 0%

commit v1 on v0

v1 whole, which is shorter than its diff:
```python
import functools

import jax
import jax.numpy as jnp
from jax import lax
from jax.experimental import pallas as pl
from jax.experimental.pallas import tpu as pltpu
from jax.sharding import PartitionSpec as P

LANES = 128
SUBS = 8
F32 = jnp.float32


def strided(ref, first, stride):
    return ref[pl.ds(first, SUBS, stride=stride), :]


def widen(src_ref, dst_ref):
    rows = 64

    @pl.loop(0, src_ref.shape[0] // rows)
    def _(i):
        at = pl.ds(pl.multiple_of(i * rows, rows), rows)
        dst_ref[at, :] = src_ref[at, :].astype(F32)


def summary_kernel(seqlen, g_ref, x_ref, lr_ref, rs_ref, send_ref, state_ref, gs, xs, acc):
    half = pl.program_id(0)
    tokens = g_ref.shape[0]
    run = tokens // SUBS
    modes = lr_ref.shape[0]
    widen(g_ref, gs)
    widen(x_ref, xs)
    rate = jnp.exp(lr_ref[...])
    zero = rate * 0.0
    some = 4
    for first in range(0, modes, some):
        decay = [
            jnp.broadcast_to(jnp.exp(-rate[m : m + 1]), (SUBS, LANES)) for m in range(first, first + some)
        ]

        def step(i, carry):
            back = run - 1 - i
            g = strided(gs, back, run)
            xb = strided(xs, back, run)
            xf = strided(xs, i, run)
            out = []
            for a, (w, q, r, l, n, f) in zip(decay, carry):
                t = a * w
                q = a * q + t
                w = t + g
                r = r + xb * w
                l = l + xb * q
                n = a * (n + xf)
                f = a * f + n
                out.append((w, q, r, l, n, f))
            return tuple(out)

        sums = lax.fori_loop(0, run, step, ((zero,) * 6,) * some, unroll=4)
        for k in range(some):
            rows = slice((first + k) * SUBS, (first + k + 1) * SUBS)
            for j in range(6):
                acc[j, rows, :] = sums[k][j]

    leap = jnp.exp(-float(run) * rate)
    w = q = res = lag = zero
    for c in range(SUBS - 1, -1, -1):
        wc, qc, rc, lc, nc, fc = (strided(acc.at[j], c, SUBS) for j in range(6))
        state_ref[pl.ds(c, SUBS, stride=SUBS), :] = w
        res = res + rc + nc * w
        lag = lag + lc + nc * q + fc * w
        q = qc + leap * (q + float(run) * w)
        w = wc + leap * w
    near = far = zero
    for c in range(SUBS):
        nc, fc = strided(acc.at[4], c, SUBS), strided(acc.at[5], c, SUBS)
        far = fc + leap * (far + float(run) * near)
        near = nc + leap * near

    span = jnp.exp(-float(tokens) * rate)
    factor = -rate * rs_ref[...] / seqlen
    parts = (w, q, near, far, res, lag, span, factor)
    slot = lax.broadcasted_iota(jnp.int32, (SUBS, LANES), 1) // 16
    for d in range(8):
        packed = zero
        for j, part in enumerate(parts):
            shift = ((j - d) * 16) % LANES
            moved = pltpu.roll(part, shift, 1) if shift else part
            packed = jnp.where(slot == j, moved, packed)
        send_ref[half * 8 + d, 16:24, :] = packed
    for d in range(16):
        send_ref[d, pl.ds(pl.multiple_of(half * 8, 8), 8), :] = w


def join_kernel(seqlen, tokens, got_ref, send_ref):
    blocks = got_ref.shape[0]

    def part(k, j):
        tile = got_ref[k, :, :]
        return pltpu.roll(tile, (-16 * j) % LANES, 1) if j else tile

    zero = jnp.zeros((SUBS, LANES), F32)
    w = q = res = lag = zero
    span = part(0, 6)
    for k in range(blocks - 1, -1, -1):
        wk, qk, nk, fk, rk, lk = (part(k, j) for j in range(6))
        res = res + rk + nk * w
        lag = lag + lk + nk * q + fk * w
        q = qk + span * (q + float(tokens) * w)
        w = wk + span * w
    lane = lax.broadcasted_iota(jnp.int32, (SUBS, LANES), 1)
    res = jnp.where(lane < 16, res * (1.0 / seqlen), 0.0)
    lag = pltpu.roll(jnp.where(lane < 16, lag * part(0, 7), 0.0), 16, 1)
    tile = res + lag
    for d in range(send_ref.shape[0]):
        send_ref[d, :, :] = tile


def input_kernel(tokens, me_ref, g_ref, lr_ref, rs_ref, got_ref, state_ref, out_ref, gs, os):
    run = tokens // SUBS
    modes = lr_ref.shape[0]
    widen(g_ref, gs)
    rate = jnp.exp(lr_ref[...])
    span = jnp.exp(-float(tokens) * rate)
    me = me_ref[0]
    enter = jnp.zeros((SUBS, LANES), F32)
    for k in range(got_ref.shape[0] - 1, 0, -1):
        enter = jnp.where(k > me, got_ref[k, :, :] + span * enter, enter)
    after = (SUBS - 1) - lax.broadcasted_iota(jnp.int32, (SUBS, LANES), 0)
    runs_left = after.astype(F32) * float(run)
    decay, resid, start = [], [], []
    for m in range(modes):
        rm = jnp.broadcast_to(rate[m : m + 1], (SUBS, LANES))
        decay.append(jnp.exp(-rm))
        resid.append(jnp.broadcast_to(rs_ref[m : m + 1, :], (SUBS, LANES)))
        start.append(state_ref[m * SUBS : (m + 1) * SUBS, :] + jnp.exp(-rm * runs_left) * enter[m : m + 1])

    def step(i, carry):
        back = run - 1 - i
        g = strided(gs, back, run)
        carry = tuple(a * w + g for a, w in zip(decay, carry))
        terms = [r * w for r, w in zip(resid, carry)]
        while len(terms) > 1:
            terms = [a + b for a, b in zip(terms[::2], terms[1::2])]
        os[pl.ds(back, SUBS, stride=run), :] = terms[0]
        return carry

    lax.fori_loop(0, run, step, tuple(start), unroll=4)
    rows = 64

    @pl.loop(0, tokens // rows)
    def _(i):
        at = pl.ds(pl.multiple_of(i * rows, rows), rows)
        out_ref[at, :] = os[at, :].astype(out_ref.dtype)


def total_kernel(got_ref, res_ref, lag_ref):
    total = got_ref[0, :, :]
    for k in range(1, got_ref.shape[0]):
        total = total + got_ref[k, :, :]
    res_ref[...] = total[:, :16]
    lag_ref[...] = total[:, 16:32]


def on_device(grad_out, conv_input, residues, log_rate):
    n_context, n_data = lax.axis_size("ctx"), lax.axis_size("dp")
    tokens, chans = grad_out.shape
    filters, modes = residues.shape
    seqlen = tokens * n_context
    halves = chans // LANES
    rate_rows, resid_rows = log_rate.T, residues.T
    column = lambda h: (0, h)
    big = pl.BlockSpec((tokens, LANES), column)
    small = pl.BlockSpec((modes, LANES), column)
    states = pl.BlockSpec((modes * SUBS, LANES), column)
    params = pltpu.CompilerParams(vmem_limit_bytes=32 * 1024 * 1024)

    send, state = pl.pallas_call(
        functools.partial(summary_kernel, float(seqlen)),
        grid=(halves,),
        in_specs=[big, big, small, small],
        out_specs=[pl.BlockSpec((n_context, 24, LANES), lambda h: (0, 0, 0)), states],
        out_shape=[
            jax.ShapeDtypeStruct((n_context, 24, LANES), F32),
            jax.ShapeDtypeStruct((modes * SUBS, chans), F32),
        ],
        scratch_shapes=[
            pltpu.VMEM((tokens, LANES), F32),
            pltpu.VMEM((tokens, LANES), F32),
            pltpu.VMEM((6, modes * SUBS, LANES), F32),
        ],
        compiler_params=params,
        name="summary",
    )(grad_out, conv_input, rate_rows, resid_rows)

    got = lax.all_to_all(send, "ctx", split_axis=0, concat_axis=0, tiled=True)

    shares = pl.pallas_call(
        functools.partial(join_kernel, float(seqlen), tokens),
        grid=(1,),
        in_specs=[pl.BlockSpec((n_context, SUBS, LANES), lambda h: (0, 2, 0))],
        out_specs=pl.BlockSpec((n_data, SUBS, LANES), lambda h: (0, 0, 0)),
        out_shape=jax.ShapeDtypeStruct((n_data, SUBS, LANES), F32),
        compiler_params=params,
        name="join",
    )(got)

    shared = lax.all_to_all(shares, "dp", split_axis=0, concat_axis=0, tiled=True)

    me = lax.axis_index("ctx").astype(jnp.int32).reshape(1)
    grad_input = pl.pallas_call(
        functools.partial(input_kernel, tokens),
        grid=(halves,),
        in_specs=[
            pl.BlockSpec(memory_space=pltpu.SMEM),
            big,
            small,
            small,
            pl.BlockSpec((n_context, SUBS, LANES), lambda h: (0, h, 0)),
            states,
        ],
        out_specs=big,
        out_shape=jax.ShapeDtypeStruct((tokens, chans), jnp.bfloat16),
        scratch_shapes=[pltpu.VMEM((tokens, LANES), F32), pltpu.VMEM((tokens, LANES), F32)],
        compiler_params=params,
        cost_estimate=pl.CostEstimate(
            flops=4 * tokens * chans * modes, bytes_accessed=4 * tokens * chans, transcendentals=0
        ),
        name="input_gradient",
    )(me, grad_out, rate_rows, resid_rows, got, state)

    whole = pl.BlockSpec((modes, 16), lambda h: (0, 0))
    grad_residue, grad_lograte = pl.pallas_call(
        total_kernel,
        grid=(1,),
        in_specs=[pl.BlockSpec((n_data, SUBS, LANES), lambda h: (0, 0, 0))],
        out_specs=[whole, whole],
        out_shape=[jax.ShapeDtypeStruct((modes, 16), F32)] * 2,
        compiler_params=params,
        name="total",
    )(shared)
    return grad_input, grad_residue.T, grad_lograte.T


def solution(mesh):
    in_specs = (P("ctx", "dp"), P("ctx", "dp"), P(), P())
    out_specs = (P("ctx", "dp"), P("ctx", None), P("ctx", None))
    return jax.shard_map(
        on_device, mesh=mesh, in_specs=in_specs, out_specs=out_specs, check_vma=False
    )
```

time: 701 us -> 67.5 us (0.10)
  waiting for transfers between devices: 268 us -> 4.37 us
  local copies, waits for them, and re-layouts: 198 us -> 4.15 us
  other arithmetic: 84.1 us -> 0 us
  blocking collectives: 70.9 us -> 33 us
  starting transfers between devices: 43.6 us -> 12.3 us
  matrix products: 15.3 us -> 0 us
  between operations: 14.3 us -> 0.7 us
  Pallas kernels: 0 us -> 12.6 us
    unnamed x4 -> x0, waiting for transfers between devices: 236 us -> none
    psum x1 -> x0, blocking collectives: 70.9 us -> none  [on_device(): grad_residue, grad_lograte = lax.psum((shares[0], shares[1]), 'dp')]
    slice x368 -> x0, local copies, waits for them, and re-layouts: 55.5 us -> none  [the longest x336 48.8 us: block_pass(): lax.associative_scan(lambda left, right: state_combine(rate, left, right)...]
    add x248 -> x0, other arithmetic: 54 us -> none  [the longest x120 52.4 us: state_combine(): w_new = decay * earlier[0] + later[0]]
    pad x192 -> x0, local copies, waits for them, and re-layouts: 34.2 us -> none  [block_pass(): lax.associative_scan(lambda left, right: state_combine(rate, left, right)...]
    all_to_all x0 -> x1, blocking collectives: none -> 33 us  [on_device(): got = lax.all_to_all(send, 'ctx', split_axis=0, concat_axis=0, tiled=True)]
    all_to_all x3 -> x1, starting transfers between devices: 43.5 us -> 12.3 us  [on_device(): lax.all_to_all(shares, 'dp', split_axis=0, concat_axis=0, tiled=True)]
    dynamic_slice x48 -> x0, local copies, waits for them, and re-layouts: 28.5 us -> none  [slab_pass(): lax.map(lambda item: block_pass(item[0], item[1], item[2], item[3], blk),...]
  transfers between devices with their start and end apart: 5 -> 1, of which waited for: 4 -> 1; matrix products, arithmetic and copies ran while one was open for 1% -> 0% of each run, Pallas kernels for 0% -> 5%
where the time goes in v1:
time: 67.5 us; the launch traced here: 67.1 us
  blocking collectives  33 us (49%)
  Pallas kernels  12.6 us (19%)
  starting transfers between devices  12.3 us (18%)
  waiting for transfers between devices  4.37 us (6%)
  local copies, waits for them, and re-layouts  4.15 us (6%)
  between operations  0.7 us (1%)
    all_to_all x1, blocking collectives, on_device(): got = lax.all_to_all(send, 'ctx', split_axis=0, concat_axis=0, tiled=True)  33 us
    all_to_all x1, starting transfers between devices, on_device(): lax.all_to_all(shares, 'dp', split_axis=0, concat_axis=0, tiled=True)  12.3 us
    pallas_call x1, Pallas kernels, on_device(): pl.pallas_call(functools.partial(summary_kernel, float(seqlen)), grid=(ha...  7.36 us
    all_to_all x1, waiting for transfers between devices, on_device(): lax.all_to_all(shares, 'dp', split_axis=0, concat_axis=0, tiled=True)  4.37 us
    unnamed x14, local copies, waits for them, and re-layouts  4.15 us
    pallas_call x1, Pallas kernels, on_device(): pl.pallas_call(functools.partial(input_kernel, tokens), grid=(halves,), i...  3.64 us
  transfers between devices with their start and end apart: 1, of which 1 were waited for; matrix products, arithmetic and copies ran while one was open for 0% of the time, Pallas kernels for 5%

profile of v1, /device:TPU:1, one launch (start us, length us, event | category | flops | bytes accessed | tf_op | source)
XLA Modules:
  0.0 67.1 jit_solution(13548627878313840228)
XLA Ops:
  0.6 0.0 copy-start
  0.6 1.0 %copy-done = bf16[1024,256]{1,0:T(8,128)(2,1)S(1)} copy-done((bf16[1024,256]{1,0:T(8,128)(2,1)S(1)}, bf16[1024,256]{1,0:T(8,128)(2,1)}, u32[]{:S(2)}) %copy-start) | copy-done | bytes 524312
  1.7 0.0 copy-start.2
  1.7 1.0 %copy-done.2 = bf16[1024,256]{1,0:T(8,128)(2,1)S(1)} copy-done((bf16[1024,256]{1,0:T(8,128)(2,1)S(1)}, bf16[1024,256]{1,0:T(8,128)(2,1)}, u32[]{:S(2)}) %copy-start.2) | copy-done | bytes 524312
  2.7 0.0 copy-start.3
  2.7 0.7 %copy-done.3 = f32[256,8]{0,1:T(8,128)S(1)} copy-done((f32[256,8]{0,1:T(8,128)S(1)}, f32[256,8]{0,1:T(8,128)}, u32[]{:S(2)}) %copy-start.3) | copy-done | bytes 8216
  3.4 0.0 copy-start.5
  3.4 0.7 %copy-done.5 = f32[256,8]{0,1:T(8,128)S(1)} copy-done((f32[256,8]{0,1:T(8,128)S(1)}, f32[256,8]{0,1:T(8,128)}, u32[]{:S(2)}) %copy-start.5) | copy-done | bytes 8216
  4.1 7.4 %summary.1 = (f32[16,24,128]{2,1,0:T(8,128)S(1)}, f32[64,256]{1,0:T(8,128)S(1)}) custom-call(bf16[1024,256]{1,0:T(8,128)(2,1)S(1)} %copy-done, bf16[1024,256]{1,0:T(8,128)(2,1)S(1)} %copy-done.2, f32[8,256]{1,0:T(8,128)S(1)} %bitcast.5, f32[8,256]{1,0:T(8,128)S(1)} %bitcast.7), custom_call_target="tpu_custom_call" | custom-call | tf_op jit(solution)/shard_map/summary/pallas_call | solution.py:179
  11.5 0.0 copy-start.1
  11.5 33.0 %all_to_all.10.got_ref = f32[16,24,128]{2,1,0:T(8,128)S(1)} all-to-all(f32[16,24,128]{2,1,0:T(8,128)S(1)} %get-tuple-element.7), channel_id=1, replica_groups=mesh['dp'=32,'ctx'=16] {'ctx'}, dimensions={0} | all-to-all | bytes 393216 | tf_op jit(solution)/shard_map/all_to_all | solution.py:197
  44.5 0.9 %join.1 = f32[32,8,128]{2,1,0:T(8,128)} custom-call(f32[16,24,128]{2,1,0:T(8,128)S(1)} %all_to_all.10.got_ref), custom_call_target="tpu_custom_call" | custom-call | tf_op jit(solution)/shard_map/join/pallas_call | solution.py:199
  45.4 0.0 copy-start.6
  45.4 12.3 %all-to-all-start.1 = ((f32[32,8,128]{2,1,0:T(8,128)}), f32[32,8,128]{2,1,0:T(8,128)S(1)}, u32[]{:S(2)}, u32[]{:S(2)}) async-start(f32[32,8,128]{2,1,0:T(8,128)} %join.1), calls=%async_computation.1 | async-start | bytes 262144 | tf_op jit(solution)/shard_map/all_to_all | solution.py:209
  57.7 0.0 copy-start.4
  57.7 0.0 copy-done.1
  57.7 0.0 copy-done.6
  57.7 0.7 copy-done.4
  58.4 3.6 %input_gradient.1 = bf16[1024,256]{1,0:T(8,128)(2,1)} custom-call(s32[1]{0:T(128)} %bitcast.me_ref, bf16[1024,256]{1,0:T(8,128)(2,1)S(1)} %copy-done.1, f32[8,256]{1,0:T(8,128)S(1)} %bitcast.6, f32[8,256]{1,0:T(8,128)S(1)} %bitcast.8, f32[16,24,128]{2,1,0:T(8,128)S(1)} %all_to_all.10.got_ref, f32[64,256]{1,0:T(8,128)S(1)} %get-tuple-element.8.state_ref), custom_call_target="tpu_custom_call" | custom-call | flops 8388608 | bytes 1048576 | tf_op jit(solution)/shard_map/input_gradient/pallas_call | solution.py:212
  62.0 4.4 %all-to-all-done.1.got_ref = f32[32,8,128]{2,1,0:T(8,128)S(1)} async-done(((f32[32,8,128]{2,1,0:T(8,128)}), f32[32,8,128]{2,1,0:T(8,128)S(1)}, u32[]{:S(2)}, u32[]{:S(2)}) %all-to-all-start.1) | async-done | bytes 131104 | tf_op jit(solution)/shard_map/all_to_all | solution.py:209
  66.4 0.7 %total.1 = (f32[8,16]{1,0:T(8,128)}, f32[8,16]{1,0:T(8,128)}) custom-call(f32[32,8,128]{2,1,0:T(8,128)S(1)} %all-to-all-done.1.got_ref), custom_call_target="tpu_custom_call" | custom-call | tf_op jit(solution)/shard_map/total/pallas_call | solution.py:234
Async XLA Ops:
  0.6 1.0 %copy-start = (bf16[1024,256]{1,0:T(8,128)(2,1)S(1)}, bf16[1024,256]{1,0:T(8,128)(2,1)}, u32[]{:S(2)}) copy-start(bf16[1024,256]{1,0:T(8,128)(2,1)} %g_ref.3) | copy-start | bytes 1572868
  1.7 1.0 %copy-start.2 = (bf16[1024,256]{1,0:T(8,128)(2,1)S(1)}, bf16[1024,256]{1,0:T(8,128)(2,1)}, u32[]{:S(2)}) copy-start(bf16[1024,256]{1,0:T(8,128)(2,1)} %x_ref.1) | copy-start | bytes 1572868
  2.7 0.7 %copy-start.3 = (f32[256,8]{0,1:T(8,128)S(1)}, f32[256,8]{0,1:T(8,128)}, u32[]{:S(2)}) copy-start(f32[256,8]{0,1:T(8,128)} %param.7) | copy-start | bytes 24580
  3.4 0.7 %copy-start.5 = (f32[256,8]{0,1:T(8,128)S(1)}, f32[256,8]{0,1:T(8,128)}, u32[]{:S(2)}) copy-start(f32[256,8]{0,1:T(8,128)} %param.6) | copy-start | bytes 24580
  11.5 46.2 %copy-start.1 = (bf16[1024,256]{1,0:T(8,128)(2,1)S(1)}, bf16[1024,256]{1,0:T(8,128)(2,1)}, u32[]{:S(2)}) copy-start(bf16[1024,256]{1,0:T(8,128)(2,1)} %g_ref.3) | copy-start | bytes 1572868
  45.4 12.3 %copy-start.6 = (f32[256,8]{0,1:T(8,128)S(1)}, f32[256,8]{0,1:T(8,128)}, u32[]{:S(2)}) copy-start(f32[256,8]{0,1:T(8,128)} %param.6) | copy-start | bytes 24580
  45.4 21.0 %all-to-all-start.1 = ((f32[32,8,128]{2,1,0:T(8,128)}), f32[32,8,128]{2,1,0:T(8,128)S(1)}, u32[]{:S(2)}, u32[]{:S(2)}) async-start(f32[32,8,128]{2,1,0:T(8,128)} %join.1), calls=%async_computation.1 | async-start | bytes 262144 | tf_op jit(solution)/shard_map/all_to_all | solution.py:209
  57.7 0.7 %copy-start.4 = (f32[256,8]{0,1:T(8,128)S(1)}, f32[256,8]{0,1:T(8,128)}, u32[]{:S(2)}) copy-start(f32[256,8]{0,1:T(8,128)} %param.7) | copy-start | bytes 24580

commit v2 on v0

v2 whole, which is shorter than its diff:
```python
import functools

import jax
import jax.numpy as jnp
from jax import lax
from jax.experimental import pallas as pl
from jax.experimental.pallas import tpu as pltpu
from jax.sharding import PartitionSpec as P

LANES = 128
SUBS = 8
OWN = 16
STEP = 4
SOME = 4
F32 = jnp.float32
BF16 = jnp.bfloat16
VMEM = pl.BlockSpec(memory_space=pltpu.VMEM)
HBM = pl.BlockSpec(memory_space=pltpu.HBM)
SMEM = pl.BlockSpec(memory_space=pltpu.SMEM)


def interleave(src_ref, dst_ref, base):
    run = src_ref.shape[0] // SUBS

    @pl.loop(0, run // 16)
    def _(i):
        for c in range(SUBS):
            rows = src_ref[pl.ds(pl.multiple_of(c * run + i * 16, 16), 16), :]
            dst_ref[pl.ds(base + i * (16 * SUBS) + c, 16, stride=SUBS), :] = rows.astype(F32)


def step_of(ref, base, b):
    size = STEP * SUBS
    rows = ref[pl.ds(pl.multiple_of(base + b * size, size), size), :]
    return [rows[j * SUBS : (j + 1) * SUBS] for j in range(STEP)]


def summary_kernel(
    seqlen, me_ref, g_hbm, x_hbm, lr_hbm, rs_hbm,
    send_ref, state_ref, wide_ref, own_ref,
    gb, xb, lr_ref, rs_ref, xs, acc, ws, packs, sems,
):
    tokens = g_hbm.shape[0]
    halves = g_hbm.shape[1] // LANES
    run = tokens // SUBS
    steps = run // STEP
    modes = lr_hbm.shape[0]

    def column(hbm, buf, half, sem):
        return pltpu.make_async_copy(hbm.at[:, pl.ds(half * LANES, LANES)], buf.at[half], sem)

    small = [
        column(hbm, buf, half, sems.at[2 * i + half])
        for i, (hbm, buf) in enumerate(((lr_hbm, lr_ref), (rs_hbm, rs_ref)))
        for half in range(halves)
    ]
    large = [
        [column(g_hbm, gb, half, sems.at[4 + half]), column(x_hbm, xb, half, sems.at[6 + half])]
        for half in range(halves)
    ]
    for copy in large[0] + small + large[1]:
        copy.start()
    for copy in small:
        copy.wait()

    for half in range(halves):
        base = half * tokens
        rate = jnp.exp(lr_ref[half])
        zero = rate * 0.0
        for copy in large[half]:
            copy.wait()
        interleave(gb.at[half], wide_ref, base)
        interleave(xb.at[half], xs, 0)

        def near_lags(i, carry):
            g0, g1, g2, g3 = step_of(wide_ref, base, i)
            x0, x1, x2, x3 = step_of(xs, 0, i)
            c0, c1, c2, c3 = carry
            return (
                c0 + ((g0 * x0 + g1 * x1) + (g2 * x2 + g3 * x3)),
                c1 + ((g1 * x0 + g2 * x1) + g3 * x2),
                c2 + (g2 * x0 + g3 * x1),
                c3 + g3 * x0,
            )

        c0, c1, c2, c3 = lax.fori_loop(0, steps, near_lags, (zero,) * 4, unroll=4)

        for first in range(0, modes, SOME):
            rows = [jnp.broadcast_to(rate[m : m + 1], (SUBS, LANES)) for m in range(first, first + SOME)]
            decay = [jnp.exp(-r) for r in rows]
            leap = [jnp.exp(-float(STEP) * r) for r in rows]

            def step(i, carry):
                b = steps - 1 - i
                g0, g1, g2, g3 = step_of(wide_ref, base, b)
                x0, x1, x2, x3 = step_of(xs, 0, b)
                out = []
                for a, a4, (w, q, r, l, n, s, e, p) in zip(decay, leap, carry):
                    y0 = a * x0
                    y1 = x1 + y0
                    y2 = x2 + a * y1
                    v = x3 + a * y2
                    dv = a * (y2 + a * (y1 + y0))
                    r = r + v * w
                    l = l + (v * q + dv * w)
                    n = n + p * v
                    s = s + n
                    e = e + p * dv
                    p = p * a4
                    h = a * g3
                    t2 = g2 + h
                    t1 = g1 + a * t2
                    u = g0 + a * t1
                    du = a * (t1 + a * (t2 + h))
                    z = a4 * w
                    q = (du + a4 * q) + float(STEP) * z
                    w = u + z
                    out.append((w, q, r, l, n, s, e, p))
                return tuple(out)

            start = (zero,) * 7 + (zero + 1.0,)
            sums = lax.fori_loop(0, steps, step, (start,) * SOME, unroll=8)
            for k in range(SOME):
                w, q, r, l, n, s, e, _ = sums[k]
                a = decay[k]
                k1, k2, k3 = a * c1, a * a * c2, a * a * a * c3
                values = (
                    w,
                    q,
                    a * r + (c0 + k1) + (k2 + k3),
                    a * (l + r) + k1 + 2.0 * k2 + 3.0 * k3,
                    a * n,
                    a * (n + e + float(STEP) * (float(steps) * n - s)),
                )
                for j in range(6):
                    acc[j, (first + k) * SUBS : (first + k + 1) * SUBS, :] = values[j]

        def of_run(j, c):
            return acc[j, pl.ds(c, modes, stride=SUBS), :]

        leap = jnp.exp(-float(run) * rate)
        w = q = res = lag = zero
        for c in range(SUBS - 1, -1, -1):
            wc, qc, rc, lc, nc, fc = (of_run(j, c) for j in range(6))
            state_ref[half, pl.ds(c, modes, stride=SUBS), :] = w
            res = res + rc + nc * w
            lag = lag + lc + nc * q + fc * w
            z = leap * w
            q = qc + leap * q + float(run) * z
            w = wc + z
        near = far = zero
        for c in range(SUBS):
            z = leap * near
            far = of_run(5, c) + leap * far + float(run) * z
            near = of_run(4, c) + z
        state_ref[half, modes * SUBS : modes * SUBS + modes, :] = rate
        state_ref[half, modes * SUBS + modes : modes * SUBS + 2 * modes, :] = rs_ref[half]

        ws[half * SUBS : (half + 1) * SUBS, :] = w
        res_high, lag_high = res.astype(BF16).astype(F32), lag.astype(BF16).astype(F32)
        parts = (w, q, near, far, res_high, lag_high, res - res_high, lag - lag_high)
        slot = lax.broadcasted_iota(jnp.int32, (SUBS, LANES), 1) // OWN
        for d in range(LANES // OWN):
            packed = zero
            for j, part in enumerate(parts):
                shift = ((j - d) * OWN) % LANES
                packed = jnp.where(slot == j, pltpu.roll(part, shift, 1) if shift else part, packed)
            packs[half * (LANES // OWN) + d, :, :] = packed

    ahead = ws[...]
    for d in range(send_ref.shape[0]):
        send_ref[d, :, :] = jnp.concatenate([ahead, packs[d]], axis=0).astype(BF16)

    me = me_ref[0]
    slots = LANES // OWN
    upper = me >= slots
    shift = jnp.where(me % slots == 0, 0, LANES - (me % slots) * OWN)
    rate = jnp.exp(pltpu.roll(jnp.where(upper, lr_ref[1], lr_ref[0]), shift, 1))
    resid = pltpu.roll(jnp.where(upper, rs_ref[1], rs_ref[0]), shift, 1)
    own_ref[0:SUBS, :] = jnp.exp(-float(tokens) * rate)
    own_ref[SUBS : 2 * SUBS, :] = -rate * resid * (1.0 / seqlen)


def join_kernel(seqlen, tokens, got_ref, own_ref, send_ref):
    blocks = got_ref.shape[0]

    def slot(tile, j):
        return pltpu.roll(tile, LANES - OWN * j, 1)

    span = own_ref[0:SUBS, :]
    w = q = res = lag = every = jnp.zeros((SUBS, LANES), F32)
    for k in range(blocks - 1, -1, -1):
        tile = got_ref[k, :, :].astype(F32)[2 * SUBS : 3 * SUBS]
        every = every + tile
        near = slot(tile, 2)
        res = res + near * w
        lag = lag + near * q + slot(tile, 3) * w
        z = span * w
        q = slot(tile, 1) + span * q + float(tokens) * z
        w = tile + z
    res = (res + (slot(every, 4) + slot(every, 6))) * (1.0 / seqlen)
    lag = (lag + (slot(every, 5) + slot(every, 7))) * own_ref[SUBS : 2 * SUBS, :]
    lane = lax.broadcasted_iota(jnp.int32, (SUBS, LANES), 1)

    def in_a_row(tile):
        tile = pltpu.roll(jnp.where(lane < OWN, tile, 0.0), 0, 1, stride=OWN, stride_axis=0)
        return jnp.sum(tile, axis=0, keepdims=True)

    rows = jnp.concatenate([in_a_row(res), in_a_row(lag)], axis=0)
    send_ref[...] = jnp.broadcast_to(rows[None], send_ref.shape)


def input_kernel(tokens, me_ref, got_ref, state_ref, wide_ref, out_hbm, os, ob, sems):
    run = tokens // SUBS
    steps = run // STEP
    halves = state_ref.shape[0]
    modes = SUBS
    me = me_ref[0]
    rates = [state_ref[half, modes * SUBS : modes * SUBS + modes, :] for half in range(halves)]
    span = jnp.exp(-float(tokens) * jnp.concatenate(rates, axis=0))
    enter = jnp.zeros_like(span)
    for k in range(got_ref.shape[0] - 1, 0, -1):
        tile = got_ref[k, :, :].astype(F32)[: halves * modes]
        enter = jnp.where(k > me, tile + span * enter, enter)
    after = (SUBS - 1) - lax.broadcasted_iota(jnp.int32, (SUBS, LANES), 0)
    runs_left = after.astype(F32) * float(run)

    def writeback(half):
        return pltpu.make_async_copy(ob.at[half], out_hbm.at[:, pl.ds(half * LANES, LANES)], sems.at[half])

    for half in range(halves):
        base = half * tokens
        decay, resid, start = [], [], []
        for m in range(modes):
            at = modes * SUBS + m
            rm = jnp.broadcast_to(state_ref[half, at : at + 1, :], (SUBS, LANES))
            decay.append(jnp.exp(-rm))
            resid.append(jnp.broadcast_to(state_ref[half, at + modes : at + modes + 1, :], (SUBS, LANES)))
            row = half * modes + m
            start.append(
                state_ref[half, m * SUBS : (m + 1) * SUBS, :] + jnp.exp(-rm * runs_left) * enter[row : row + 1]
            )

        def step(i, carry):
            b = steps - 1 - i
            values = step_of(wide_ref, base, b)
            sums = [None] * STEP
            for j in range(STEP - 1, -1, -1):
                carry = tuple(a * w + values[j] for a, w in zip(decay, carry))
                terms = [r * w for r, w in zip(resid, carry)]
                while len(terms) > 1:
                    terms = [a + b for a, b in zip(terms[::2], terms[1::2])]
                sums[j] = terms[0]
            size = STEP * SUBS
            os[pl.ds(pl.multiple_of(b * size, size), size), :] = jnp.concatenate(sums, axis=0)
            return carry

        lax.fori_loop(0, steps, step, tuple(start), unroll=2)

        @pl.loop(0, run // 16)
        def _(i):
            for c in range(SUBS):
                rows = os[pl.ds(i * (16 * SUBS) + c, 16, stride=SUBS), :]
                ob[half, pl.ds(pl.multiple_of(c * run + i * 16, 16), 16), :] = rows.astype(BF16)

        writeback(half).start()
    for half in range(halves):
        writeback(half).wait()


def total_kernel(got_ref, res_ref, lag_ref):
    total = got_ref[0, :, :]
    for k in range(1, got_ref.shape[0]):
        total = total + got_ref[k, :, :]
    mode = lax.broadcasted_iota(jnp.int32, (SUBS, LANES), 0)
    for j, out in enumerate((res_ref, lag_ref)):
        row = jnp.broadcast_to(total[j : j + 1], (SUBS, LANES))
        tile = row
        for m in range(1, SUBS):
            tile = jnp.where(mode == m, pltpu.roll(row, LANES - OWN * m, 1), tile)
        out[...] = tile[:, :OWN]


def on_device(grad_out, conv_input, residues, log_rate):
    n_context, n_data = lax.axis_size("ctx"), lax.axis_size("dp")
    tokens, chans = grad_out.shape
    modes = residues.shape[1]
    seqlen = tokens * n_context
    halves = chans // LANES
    me = lax.axis_index("ctx").astype(jnp.int32).reshape(1)
    params = pltpu.CompilerParams(vmem_limit_bytes=24 * 1024 * 1024)

    send, state, wide, own = pl.pallas_call(
        functools.partial(summary_kernel, float(seqlen)),
        in_specs=[SMEM, HBM, HBM, HBM, HBM],
        out_specs=[VMEM, VMEM, VMEM, VMEM],
        out_shape=[
            jax.ShapeDtypeStruct((n_context, 3 * SUBS, LANES), BF16),
            jax.ShapeDtypeStruct((halves, modes * SUBS + 2 * modes, LANES), F32),
            jax.ShapeDtypeStruct((halves * tokens, LANES), F32),
            jax.ShapeDtypeStruct((2 * SUBS, LANES), F32),
        ],
        scratch_shapes=[
            pltpu.VMEM((halves, tokens, LANES), BF16),
            pltpu.VMEM((halves, tokens, LANES), BF16),
            pltpu.VMEM((halves, modes, LANES), F32),
            pltpu.VMEM((halves, modes, LANES), F32),
            pltpu.VMEM((tokens, LANES), F32),
            pltpu.VMEM((6, modes * SUBS, LANES), F32),
            pltpu.VMEM((halves * modes, LANES), F32),
            pltpu.VMEM((n_context, modes, LANES), F32),
            pltpu.SemaphoreType.DMA((8,)),
        ],
        compiler_params=params,
        name="summary",
    )(me, *(
        pltpu.with_memory_space_constraint(array, pltpu.HBM)
        for array in (grad_out, conv_input, log_rate.T, residues.T)
    ))

    got = lax.all_to_all(send, "ctx", split_axis=0, concat_axis=0, tiled=True)

    shares = pl.pallas_call(
        functools.partial(join_kernel, float(seqlen), tokens),
        in_specs=[VMEM, VMEM],
        out_specs=VMEM,
        out_shape=jax.ShapeDtypeStruct((n_data, 2, LANES), F32),
        compiler_params=params,
        name="join",
    )(got, own)

    shared = lax.all_to_all(shares, "dp", split_axis=0, concat_axis=0, tiled=True)

    grad_input = pl.pallas_call(
        functools.partial(input_kernel, tokens),
        in_specs=[SMEM, VMEM, VMEM, VMEM],
        out_specs=HBM,
        out_shape=jax.ShapeDtypeStruct((tokens, chans), BF16),
        scratch_shapes=[
            pltpu.VMEM((tokens, LANES), F32),
            pltpu.VMEM((halves, tokens, LANES), BF16),
            pltpu.SemaphoreType.DMA((2,)),
        ],
        compiler_params=params,
        cost_estimate=pl.CostEstimate(
            flops=4 * tokens * chans * modes, bytes_accessed=4 * tokens * chans, transcendentals=0
        ),
        name="input_gradient",
    )(me, got, state, wide)

    grad_residue, grad_lograte = pl.pallas_call(
        total_kernel,
        in_specs=[VMEM],
        out_specs=[VMEM, VMEM],
        out_shape=[jax.ShapeDtypeStruct((modes, OWN), F32)] * 2,
        compiler_params=params,
        name="total",
    )(shared)
    return grad_input, grad_residue.T, grad_lograte.T


def solution(mesh):
    in_specs = (P("ctx", "dp"), P("ctx", "dp"), P(), P())
    out_specs = (P("ctx", "dp"), P("ctx", None), P("ctx", None))
    return jax.shard_map(
        on_device, mesh=mesh, in_specs=in_specs, out_specs=out_specs, check_vma=False
    )
```

time: 701 us -> 56.2 us (0.08)
  waiting for transfers between devices: 268 us -> 5.23 us
  local copies, waits for them, and re-layouts: 198 us -> 0 us
  other arithmetic: 84.1 us -> 0 us
  blocking collectives: 70.9 us -> 32.1 us
  starting transfers between devices: 43.6 us -> 9.17 us
  matrix products: 15.3 us -> 0 us
  between operations: 14.3 us -> 0.66 us
  Pallas kernels: 0 us -> 8.88 us
    unnamed x4 -> x0, waiting for transfers between devices: 236 us -> none
    psum x1 -> x0, blocking collectives: 70.9 us -> none  [on_device(): grad_residue, grad_lograte = lax.psum((shares[0], shares[1]), 'dp')]
    slice x368 -> x0, local copies, waits for them, and re-layouts: 55.5 us -> none  [the longest x336 48.8 us: block_pass(): lax.associative_scan(lambda left, right: state_combine(rate, left, right)...]
    add x248 -> x0, other arithmetic: 54 us -> none  [the longest x120 52.4 us: state_combine(): w_new = decay * earlier[0] + later[0]]
    all_to_all x3 -> x1, starting transfers between devices: 43.5 us -> 9.17 us  [on_device(): lax.all_to_all(shares, 'dp', split_axis=0, concat_axis=0, tiled=True)]
    pad x192 -> x0, local copies, waits for them, and re-layouts: 34.2 us -> none  [block_pass(): lax.associative_scan(lambda left, right: state_combine(rate, left, right)...]
    all_to_all x0 -> x1, blocking collectives: none -> 32.1 us  [on_device(): got = lax.all_to_all(send, 'ctx', split_axis=0, concat_axis=0, tiled=True)]
    dynamic_slice x48 -> x0, local copies, waits for them, and re-layouts: 28.5 us -> none  [slab_pass(): lax.map(lambda item: block_pass(item[0], item[1], item[2], item[3], blk),...]
  transfers between devices with their start and end apart: 5 -> 1, of which waited for: 4 -> 1; matrix products, arithmetic and copies ran while one was open for 1% -> 0% of each run, Pallas kernels for 0% -> 4%
where the time goes in v2:
time: 56.2 us; the launch traced here: 56 us
  blocking collectives  32.1 us (57%)
  starting transfers between devices  9.17 us (16%)
  Pallas kernels  8.88 us (16%)
  waiting for transfers between devices  5.23 us (9%)
  between operations  0.66 us (1%)
    all_to_all x1, blocking collectives, on_device(): got = lax.all_to_all(send, 'ctx', split_axis=0, concat_axis=0, tiled=True)  32.1 us
    all_to_all x1, starting transfers between devices, on_device(): lax.all_to_all(shares, 'dp', split_axis=0, concat_axis=0, tiled=True)  9.17 us
    all_to_all x1, waiting for transfers between devices, on_device(): lax.all_to_all(shares, 'dp', split_axis=0, concat_axis=0, tiled=True)  5.23 us
    pallas_call x1, Pallas kernels, on_device(): pl.pallas_call(functools.partial(summary_kernel, float(seqlen)), in_specs...  5.09 us
    pallas_call x1, Pallas kernels, on_device(): pl.pallas_call(functools.partial(input_kernel, tokens), in_specs=[SMEM, V...  2.28 us
  transfers between devices with their start and end apart: 1, of which 1 were waited for; matrix products, arithmetic and copies ran while one was open for 0% of the time, Pallas kernels for 4%

profile of v2, /device:TPU:1, one launch (start us, length us, event | category | flops | bytes accessed | tf_op | source)
XLA Modules:
  0.0 56.0 jit_solution(9856784723314551796)
XLA Ops:
  0.6 5.1 %summary.1 = (bf16[16,24,128]{2,1,0:T(8,128)(2,1)S(1)}, f32[2,80,128]{2,1,0:T(8,128)S(1)}, f32[2048,128]{1,0:T(8,128)S(1)}, f32[16,128]{1,0:T(8,128)S(1)}) custom-call(s32[1]{0:T(128)} %bitcast.me_ref, bf16[1024,256]{1,0:T(8,128)(2,1)} %g_hbm.1, bf16[1024,256]{1,0:T(8,128)(2,1)} %x_hbm.1, f32[8,256]{1,0:T(8,128)} %bitcast.5, f32[8,256]{1,0:T(8,128)} %bitcast.6), custom_call_target="tpu_custom_call" | custom-call | tf_op jit(solution)/shard_map/summary/pallas_call | solution.py:293
  5.7 32.1 %all_to_all.10.got_ref = bf16[16,24,128]{2,1,0:T(8,128)(2,1)S(1)} all-to-all(bf16[16,24,128]{2,1,0:T(8,128)(2,1)S(1)} %get-tuple-element.9), channel_id=1, replica_groups=mesh['dp'=32,'ctx'=16] {'ctx'}, dimensions={0} | all-to-all | bytes 196608 | tf_op jit(solution)/shard_map/all_to_all | solution.py:321
  37.8 0.8 %join.1 = f32[32,2,128]{2,1,0:T(2,128)} custom-call(bf16[16,24,128]{2,1,0:T(8,128)(2,1)S(1)} %all_to_all.10.got_ref, f32[16,128]{1,0:T(8,128)S(1)} %get-tuple-element.12.own_ref), custom_call_target="tpu_custom_call" | custom-call | tf_op jit(solution)/shard_map/join/pallas_call | solution.py:323
  38.6 9.2 %all-to-all-start.1 = ((f32[32,2,128]{2,1,0:T(2,128)}), f32[32,2,128]{2,1,0:T(2,128)S(1)}, u32[]{:S(2)}, u32[]{:S(2)}) async-start(f32[32,2,128]{2,1,0:T(2,128)} %join.1), calls=%async_computation.1 | async-start | bytes 65536 | tf_op jit(solution)/shard_map/all_to_all | solution.py:332
  47.8 2.3 %input_gradient.1 = bf16[1024,256]{1,0:T(8,128)(2,1)} custom-call(s32[1]{0:T(128)} %bitcast.me_ref, bf16[16,24,128]{2,1,0:T(8,128)(2,1)S(1)} %all_to_all.10.got_ref, f32[2,80,128]{2,1,0:T(8,128)S(1)} %get-tuple-element.10.state_ref, f32[2048,128]{1,0:T(8,128)S(1)} %get-tuple-element.11.wide_ref), custom_call_target="tpu_custom_call" | custom-call | flops 8388608 | bytes 1048576 | tf_op jit(solution)/shard_map/input_gradient/pallas_call | solution.py:334
  50.1 5.2 %all-to-all-done.1.got_ref = f32[32,2,128]{2,1,0:T(2,128)S(1)} async-done(((f32[32,2,128]{2,1,0:T(2,128)}), f32[32,2,128]{2,1,0:T(2,128)S(1)}, u32[]{:S(2)}, u32[]{:S(2)}) %all-to-all-start.1) | async-done | bytes 32800 | tf_op jit(solution)/shard_map/all_to_all | solution.py:332
  55.3 0.7 %total.1 = (f32[8,16]{1,0:T(8,128)}, f32[8,16]{1,0:T(8,128)}) custom-call(f32[32,2,128]{2,1,0:T(2,128)S(1)} %all-to-all-done.1.got_ref), custom_call_target="tpu_custom_call" | custom-call | tf_op jit(solution)/shard_map/total/pallas_call | solution.py:351
Async XLA Ops:
  38.6 16.7 %all-to-all-start.1 = ((f32[32,2,128]{2,1,0:T(2,128)}), f32[32,2,128]{2,1,0:T(2,128)S(1)}, u32[]{:S(2)}, u32[]{:S(2)}) async-start(f32[32,2,128]{2,1,0:T(2,128)} %join.1), calls=%async_computation.1 | async-start | bytes 65536 | tf_op jit(solution)/shard_map/all_to_all | solution.py:332

commit v3 on v2

--- a/solution.py
+++ b/solution.py
@@ -12,6 +12,8 @@
 OWN = 16
 STEP = 4
 SOME = 4
+CTX_ORDER = [10, 0, 1, 3, 2, 4, 12, 5, 7, 13, 15, 6, 14, 8, 9, 11]
+DP_ORDER = [21, 22, 23, 24, 25, 26, 27, 28, 29, 30, 31, 0, 1, 2, 3, 4, 5, 6, 7, 8, 9, 10, 11, 12, 13, 14, 15, 16, 17, 18, 19, 20]
 F32 = jnp.float32
 BF16 = jnp.bfloat16
 VMEM = pl.BlockSpec(memory_space=pltpu.VMEM)
@@ -168,8 +170,8 @@
             packs[half * (LANES // OWN) + d, :, :] = packed
 
     ahead = ws[...]
-    for d in range(send_ref.shape[0]):
-        send_ref[d, :, :] = jnp.concatenate([ahead, packs[d]], axis=0).astype(BF16)
+    for place, d in enumerate(CTX_ORDER):
+        send_ref[place, :, :] = jnp.concatenate([ahead, packs[d]], axis=0).astype(BF16)
 
     me = me_ref[0]
     slots = LANES // OWN
@@ -190,7 +192,7 @@
     span = own_ref[0:SUBS, :]
     w = q = res = lag = every = jnp.zeros((SUBS, LANES), F32)
     for k in range(blocks - 1, -1, -1):
-        tile = got_ref[k, :, :].astype(F32)[2 * SUBS : 3 * SUBS]
+        tile = got_ref[CTX_ORDER.index(k), :, :].astype(F32)[2 * SUBS : 3 * SUBS]
         every = every + tile
         near = slot(tile, 2)
         res = res + near * w
@@ -220,7 +222,7 @@
     span = jnp.exp(-float(tokens) * jnp.concatenate(rates, axis=0))
     enter = jnp.zeros_like(span)
     for k in range(got_ref.shape[0] - 1, 0, -1):
-        tile = got_ref[k, :, :].astype(F32)[: halves * modes]
+        tile = got_ref[CTX_ORDER.index(k), :, :].astype(F32)[: halves * modes]
         enter = jnp.where(k > me, tile + span * enter, enter)
     after = (SUBS - 1) - lax.broadcasted_iota(jnp.int32, (SUBS, LANES), 0)
     runs_left = after.astype(F32) * float(run)
@@ -279,6 +281,12 @@
         for m in range(1, SUBS):
             tile = jnp.where(mode == m, pltpu.roll(row, LANES - OWN * m, 1), tile)
         out[...] = tile[:, :OWN]
+
+
+def exchange(blocks, axis, order):
+    return lax.all_to_all(
+        blocks, axis, split_axis=0, concat_axis=0, axis_index_groups=[order], tiled=True
+    )
 
 
 def on_device(grad_out, conv_input, residues, log_rate):
@@ -318,7 +326,7 @@
         for array in (grad_out, conv_input, log_rate.T, residues.T)
     ))
 
-    got = lax.all_to_all(send, "ctx", split_axis=0, concat_axis=0, tiled=True)
+    got = exchange(send, "ctx", CTX_ORDER)
 
     shares = pl.pallas_call(
         functools.partial(join_kernel, float(seqlen), tokens),
@@ -329,7 +337,7 @@
         name="join",
     )(got, own)
 
-    shared = lax.all_to_all(shares, "dp", split_axis=0, concat_axis=0, tiled=True)
+    shared = exchange(shares, "dp", DP_ORDER)
 
     grad_input = pl.pallas_call(
         functools.partial(input_kernel, tokens),

time: 56.2 us -> 44.4 us (0.79)
  blocking collectives: 32.1 us -> 24.4 us
  waiting for transfers between devices: 5.23 us -> 0.94 us
    all_to_all x1, blocking collectives: 32.1 us -> 24.4 us  [exchange(): lax.all_to_all(blocks, axis, split_axis=0, concat_axis=0, axis_index_grou...]
    all_to_all x1, waiting for transfers between devices: 5.23 us -> 0.94 us  [exchange(): lax.all_to_all(blocks, axis, split_axis=0, concat_axis=0, axis_index_grou...]
  transfers between devices with their start and end apart: 1 -> 1, of which waited for: 1 -> 1; matrix products, arithmetic and copies ran while one was open for 0% -> 0% of each run, Pallas kernels for 4% -> 5%
where the time goes in v3:
time: 44.4 us; the launch traced here: 44.2 us
  blocking collectives  24.4 us (55%)
  starting transfers between devices  9.31 us (21%)
  Pallas kernels  8.88 us (20%)
  waiting for transfers between devices  0.94 us (2%)
  between operations  0.66 us (1%)
    all_to_all x1, blocking collectives, exchange(): lax.all_to_all(blocks, axis, split_axis=0, concat_axis=0, axis_index_grou...  24.4 us
    all_to_all x1, starting transfers between devices, exchange(): lax.all_to_all(blocks, axis, split_axis=0, concat_axis=0, axis_index_grou...  9.31 us
    pallas_call x1, Pallas kernels, on_device(): pl.pallas_call(functools.partial(summary_kernel, float(seqlen)), in_specs...  5.09 us
    pallas_call x1, Pallas kernels, on_device(): pl.pallas_call(functools.partial(input_kernel, tokens), in_specs=[SMEM, V...  2.28 us
    all_to_all x1, waiting for transfers between devices, exchange(): lax.all_to_all(blocks, axis, split_axis=0, concat_axis=0, axis_index_grou...  0.94 us
  transfers between devices with their start and end apart: 1, of which 1 were waited for; matrix products, arithmetic and copies ran while one was open for 0% of the time, Pallas kernels for 5%

profile of v3, /device:TPU:1, one launch (start us, length us, event | category | flops | bytes accessed | tf_op | source)
XLA Modules:
  0.0 44.2 jit_solution(11588245621195937562)
XLA Ops:
  0.6 5.1 %summary.1 = (bf16[16,24,128]{2,1,0:T(8,128)(2,1)S(1)}, f32[2,80,128]{2,1,0:T(8,128)S(1)}, f32[2048,128]{1,0:T(8,128)S(1)}, f32[16,128]{1,0:T(8,128)S(1)}) custom-call(s32[1]{0:T(128)} %bitcast.me_ref, bf16[1024,256]{1,0:T(8,128)(2,1)} %g_hbm.1, bf16[1024,256]{1,0:T(8,128)(2,1)} %x_hbm.1, f32[8,256]{1,0:T(8,128)} %bitcast.5, f32[8,256]{1,0:T(8,128)} %bitcast.6), custom_call_target="tpu_custom_call" | custom-call | tf_op jit(solution)/shard_map/summary/pallas_call | solution.py:301
  5.7 24.4 %all_to_all.10.got_ref = bf16[16,24,128]{2,1,0:T(8,128)(2,1)S(1)} all-to-all(bf16[16,24,128]{2,1,0:T(8,128)(2,1)S(1)} %get-tuple-element.9), channel_id=1, replica_groups={{10,0,1,3,2,4,12,5,7,13,15,6,14,8,9,11},{26,16,17,19,18,20,28,21,23,29,..., dimensions={0} | all-to-all | bytes 196608 | tf_op jit(solution)/shard_map/all_to_all | solution.py:287
  30.2 0.8 %join.1 = f32[32,2,128]{2,1,0:T(2,128)} custom-call(bf16[16,24,128]{2,1,0:T(8,128)(2,1)S(1)} %all_to_all.10.got_ref, f32[16,128]{1,0:T(8,128)S(1)} %get-tuple-element.12.own_ref), custom_call_target="tpu_custom_call" | custom-call | tf_op jit(solution)/shard_map/join/pallas_call | solution.py:331
  31.0 9.3 %all-to-all-start.1 = ((f32[32,2,128]{2,1,0:T(2,128)}), f32[32,2,128]{2,1,0:T(2,128)S(1)}, u32[]{:S(2)}, u32[]{:S(2)}) async-start(f32[32,2,128]{2,1,0:T(2,128)} %join.1), calls=%async_computation.1 | async-start | bytes 65536 | tf_op jit(solution)/shard_map/all_to_all | solution.py:287
  40.3 2.3 %input_gradient.1 = bf16[1024,256]{1,0:T(8,128)(2,1)} custom-call(s32[1]{0:T(128)} %bitcast.me_ref, bf16[16,24,128]{2,1,0:T(8,128)(2,1)S(1)} %all_to_all.10.got_ref, f32[2,80,128]{2,1,0:T(8,128)S(1)} %get-tuple-element.10.state_ref, f32[2048,128]{1,0:T(8,128)S(1)} %get-tuple-element.11.wide_ref), custom_call_target="tpu_custom_call" | custom-call | flops 8388608 | bytes 1048576 | tf_op jit(solution)/shard_map/input_gradient/pallas_call | solution.py:342
  42.6 0.9 %all-to-all-done.1.got_ref = f32[32,2,128]{2,1,0:T(2,128)S(1)} async-done(((f32[32,2,128]{2,1,0:T(2,128)}), f32[32,2,128]{2,1,0:T(2,128)S(1)}, u32[]{:S(2)}, u32[]{:S(2)}) %all-to-all-start.1) | async-done | bytes 32800 | tf_op jit(solution)/shard_map/all_to_all | solution.py:287
  43.5 0.7 %total.1 = (f32[8,16]{1,0:T(8,128)}, f32[8,16]{1,0:T(8,128)}) custom-call(f32[32,2,128]{2,1,0:T(2,128)S(1)} %all-to-all-done.1.got_ref), custom_call_target="tpu_custom_call" | custom-call | tf_op jit(solution)/shard_map/total/pallas_call | solution.py:359
Async XLA Ops:
  31.0 12.5 %all-to-all-start.1 = ((f32[32,2,128]{2,1,0:T(2,128)}), f32[32,2,128]{2,1,0:T(2,128)S(1)}, u32[]{:S(2)}, u32[]{:S(2)}) async-start(f32[32,2,128]{2,1,0:T(2,128)} %join.1), calls=%async_computation.1 | async-start | bytes 65536 | tf_op jit(solution)/shard_map/all_to_all | solution.py:287

commit v4 on v3

--- a/solution.py
+++ b/solution.py
@@ -11,7 +11,7 @@
 SUBS = 8
 OWN = 16
 STEP = 4
-SOME = 4
+SOME = 2
 CTX_ORDER = [10, 0, 1, 3, 2, 4, 12, 5, 7, 13, 15, 6, 14, 8, 9, 11]
 DP_ORDER = [21, 22, 23, 24, 25, 26, 27, 28, 29, 30, 31, 0, 1, 2, 3, 4, 5, 6, 7, 8, 9, 10, 11, 12, 13, 14, 15, 16, 17, 18, 19, 20]
 F32 = jnp.float32
@@ -40,7 +40,7 @@
 def summary_kernel(
     seqlen, me_ref, g_hbm, x_hbm, lr_hbm, rs_hbm,
     send_ref, state_ref, wide_ref, own_ref,
-    gb, xb, lr_ref, rs_ref, xs, acc, ws, packs, sems,
+    gb, xb, lr_ref, rs_ref, xs, acc, sems,
 ):
     tokens = g_hbm.shape[0]
     halves = g_hbm.shape[1] // LANES
@@ -60,36 +60,25 @@
         [column(g_hbm, gb, half, sems.at[4 + half]), column(x_hbm, xb, half, sems.at[6 + half])]
         for half in range(halves)
     ]
-    for copy in large[0] + small + large[1]:
+    for copy in large[0] + small:
         copy.start()
-    for copy in small:
-        copy.wait()
-
-    for half in range(halves):
+
+    def scan(half):
         base = half * tokens
+        for copy, src, dst, at in zip(large[half], (gb, xb), (wide_ref, xs), (base, 0)):
+            copy.wait()
+            interleave(src.at[half], dst, at)
+        if half == 0:
+            for copy in large[1]:
+                copy.start()
+            for copy in small:
+                copy.wait()
         rate = jnp.exp(lr_ref[half])
         zero = rate * 0.0
-        for copy in large[half]:
-            copy.wait()
-        interleave(gb.at[half], wide_ref, base)
-        interleave(xb.at[half], xs, 0)
-
-        def near_lags(i, carry):
-            g0, g1, g2, g3 = step_of(wide_ref, base, i)
-            x0, x1, x2, x3 = step_of(xs, 0, i)
-            c0, c1, c2, c3 = carry
-            return (
-                c0 + ((g0 * x0 + g1 * x1) + (g2 * x2 + g3 * x3)),
-                c1 + ((g1 * x0 + g2 * x1) + g3 * x2),
-                c2 + (g2 * x0 + g3 * x1),
-                c3 + g3 * x0,
-            )
-
-        c0, c1, c2, c3 = lax.fori_loop(0, steps, near_lags, (zero,) * 4, unroll=4)
-
         for first in range(0, modes, SOME):
             rows = [jnp.broadcast_to(rate[m : m + 1], (SUBS, LANES)) for m in range(first, first + SOME)]
             decay = [jnp.exp(-r) for r in rows]
+            part = [a * (1.0 / STEP) for a in decay]
             leap = [jnp.exp(-float(STEP) * r) for r in rows]
 
             def step(i, carry):
@@ -97,81 +86,102 @@
                 g0, g1, g2, g3 = step_of(wide_ref, base, b)
                 x0, x1, x2, x3 = step_of(xs, 0, b)
                 out = []
-                for a, a4, (w, q, r, l, n, s, e, p) in zip(decay, leap, carry):
+                for a, a_part, a4, (w, q, r, l, n, f, p) in zip(decay, part, leap, carry):
                     y0 = a * x0
                     y1 = x1 + y0
                     y2 = x2 + a * y1
                     v = x3 + a * y2
-                    dv = a * (y2 + a * (y1 + y0))
+                    dv = a_part * (y2 + a * (y1 + y0))
                     r = r + v * w
                     l = l + (v * q + dv * w)
                     n = n + p * v
-                    s = s + n
-                    e = e + p * dv
+                    f = f + (p * dv - n)
                     p = p * a4
                     h = a * g3
                     t2 = g2 + h
                     t1 = g1 + a * t2
                     u = g0 + a * t1
-                    du = a * (t1 + a * (t2 + h))
+                    du = a_part * (t1 + a * (t2 + h))
                     z = a4 * w
-                    q = (du + a4 * q) + float(STEP) * z
+                    q = (du + a4 * q) + z
                     w = u + z
-                    out.append((w, q, r, l, n, s, e, p))
+                    out.append((w, q, r, l, n, f, p))
+                if first == 0:
+                    c0, c1, c2, c3 = carry[SOME]
+                    out.append((
+                        c0 + ((g0 * x0 + g1 * x1) + (g2 * x2 + g3 * x3)),
+                        c1 + ((g1 * x0 + g2 * x1) + g3 * x2),
+                        c2 + (g2 * x0 + g3 * x1),
+                        c3 + g3 * x0,
+                    ))
                 return tuple(out)
 
-            start = (zero,) * 7 + (zero + 1.0,)
-            sums = lax.fori_loop(0, steps, step, (start,) * SOME, unroll=8)
+            start = ((zero,) * 6 + (zero + 1.0,),) * SOME
+            if first == 0:
+                start = start + ((zero,) * 4,)
+            sums = lax.fori_loop(0, steps, step, start, unroll=16)
+            if first == 0:
+                c0, c1, c2, c3 = sums[SOME]
             for k in range(SOME):
-                w, q, r, l, n, s, e, _ = sums[k]
+                w, q, r, l, n, f, _ = sums[k]
                 a = decay[k]
                 k1, k2, k3 = a * c1, a * a * c2, a * a * a * c3
                 values = (
                     w,
-                    q,
+                    float(STEP) * q,
                     a * r + (c0 + k1) + (k2 + k3),
-                    a * (l + r) + k1 + 2.0 * k2 + 3.0 * k3,
+                    a * (float(STEP) * l + r) + k1 + 2.0 * k2 + 3.0 * k3,
                     a * n,
-                    a * (n + e + float(STEP) * (float(steps) * n - s)),
+                    a * (n + float(STEP) * (f + float(steps) * n)),
                 )
                 for j in range(6):
-                    acc[j, (first + k) * SUBS : (first + k + 1) * SUBS, :] = values[j]
-
-        def of_run(j, c):
-            return acc[j, pl.ds(c, modes, stride=SUBS), :]
-
-        leap = jnp.exp(-float(run) * rate)
-        w = q = res = lag = zero
-        for c in range(SUBS - 1, -1, -1):
-            wc, qc, rc, lc, nc, fc = (of_run(j, c) for j in range(6))
-            state_ref[half, pl.ds(c, modes, stride=SUBS), :] = w
-            res = res + rc + nc * w
-            lag = lag + lc + nc * q + fc * w
-            z = leap * w
-            q = qc + leap * q + float(run) * z
-            w = wc + z
-        near = far = zero
-        for c in range(SUBS):
-            z = leap * near
-            far = of_run(5, c) + leap * far + float(run) * z
-            near = of_run(4, c) + z
-        state_ref[half, modes * SUBS : modes * SUBS + modes, :] = rate
+                    acc[half, j, (first + k) * SUBS : (first + k + 1) * SUBS, :] = values[j]
+
+    both = range(halves)
+    for half in both:
+        scan(half)
+
+    def of_run(j, c):
+        return [acc[half, j, pl.ds(c, modes, stride=SUBS), :] for half in both]
+
+    def each(rule, *columns):
+        return [rule(*values) for values in zip(*columns)]
+
+    rate = [jnp.exp(lr_ref[half]) for half in both]
+    leap = each(lambda r: jnp.exp(-float(run) * r), rate)
+    w = q = res = lag = near = far = each(lambda r: r * 0.0, rate)
+    for i in range(SUBS):
+        c = SUBS - 1 - i
+        wc, qc, rc, lc, nc, fc = (of_run(j, c) for j in range(6))
+        for half in both:
+            state_ref[half, pl.ds(c, modes, stride=SUBS), :] = w[half]
+        res = each(lambda t, r, n, w: t + r + n * w, res, rc, nc, w)
+        lag = each(lambda t, l, n, f, w, q: t + l + (n * q + f * w), lag, lc, nc, fc, w, q)
+        z = each(lambda a, w: a * w, leap, w)
+        q = each(lambda qc, a, q, z: qc + a * q + float(run) * z, qc, leap, q, z)
+        w = each(lambda wc, z: wc + z, wc, z)
+        nc, fc = of_run(4, i), of_run(5, i)
+        z = each(lambda a, n: a * n, leap, near)
+        far = each(lambda fc, a, f, z: fc + a * f + float(run) * z, fc, leap, far, z)
+        near = each(lambda nc, z: nc + z, nc, z)
+
+    slot = lax.broadcasted_iota(jnp.int32, (SUBS, LANES), 1) // OWN
+    ahead = jnp.concatenate(w, axis=0)
+    for half in both:
+        state_ref[half, modes * SUBS : modes * SUBS + modes, :] = rate[half]
         state_ref[half, modes * SUBS + modes : modes * SUBS + 2 * modes, :] = rs_ref[half]
-
-        ws[half * SUBS : (half + 1) * SUBS, :] = w
-        res_high, lag_high = res.astype(BF16).astype(F32), lag.astype(BF16).astype(F32)
-        parts = (w, q, near, far, res_high, lag_high, res - res_high, lag - lag_high)
-        slot = lax.broadcasted_iota(jnp.int32, (SUBS, LANES), 1) // OWN
+        res_high, lag_high = res[half].astype(BF16).astype(F32), lag[half].astype(BF16).astype(F32)
+        parts = (
+            w[half], q[half], near[half], far[half],
+            res_high, lag_high, res[half] - res_high, lag[half] - lag_high,
+        )
         for d in range(LANES // OWN):
-            packed = zero
+            packed = parts[d]
             for j, part in enumerate(parts):
-                shift = ((j - d) * OWN) % LANES
-                packed = jnp.where(slot == j, pltpu.roll(part, shift, 1) if shift else part, packed)
-            packs[half * (LANES // OWN) + d, :, :] = packed
-
-    ahead = ws[...]
-    for place, d in enumerate(CTX_ORDER):
-        send_ref[place, :, :] = jnp.concatenate([ahead, packs[d]], axis=0).astype(BF16)
+                if j != d:
+                    packed = jnp.where(slot == j, pltpu.roll(part, ((j - d) * OWN) % LANES, 1), packed)
+            place = CTX_ORDER.index(half * (LANES // OWN) + d)
+            send_ref[place, :, :] = jnp.concatenate([ahead, packed], axis=0).astype(BF16)
 
     me = me_ref[0]
     slots = LANES // OWN
@@ -314,9 +324,7 @@
             pltpu.VMEM((halves, modes, LANES), F32),
             pltpu.VMEM((halves, modes, LANES), F32),
             pltpu.VMEM((tokens, LANES), F32),
-            pltpu.VMEM((6, modes * SUBS, LANES), F32),
-            pltpu.VMEM((halves * modes, LANES), F32),
-            pltpu.VMEM((n_context, modes, LANES), F32),
+            pltpu.VMEM((halves, 6, modes * SUBS, LANES), F32),
             pltpu.SemaphoreType.DMA((8,)),
         ],
         compiler_params=params,

time: 44.4 us -> 44 us (level)
  no operation moved by 1% of the time
where the time goes in v4:
time: 44 us; the launch traced here: 43.8 us
  blocking collectives  24.4 us (55%)
  starting transfers between devices  9.31 us (21%)
  Pallas kernels  8.46 us (19%)
  waiting for transfers between devices  0.94 us (2%)
  between operations  0.66 us (2%)
    all_to_all x1, blocking collectives, exchange(): lax.all_to_all(blocks, axis, split_axis=0, concat_axis=0, axis_index_grou...  24.4 us
    all_to_all x1, starting transfers between devices, exchange(): lax.all_to_all(blocks, axis, split_axis=0, concat_axis=0, axis_index_grou...  9.31 us
    pallas_call x1, Pallas kernels, on_device(): pl.pallas_call(functools.partial(summary_kernel, float(seqlen)), in_specs...  4.67 us
    pallas_call x1, Pallas kernels, on_device(): pl.pallas_call(functools.partial(input_kernel, tokens), in_specs=[SMEM, V...  2.28 us
    all_to_all x1, waiting for transfers between devices, exchange(): lax.all_to_all(blocks, axis, split_axis=0, concat_axis=0, axis_index_grou...  0.94 us
  transfers between devices with their start and end apart: 1, of which 1 were waited for; matrix products, arithmetic and copies ran while one was open for 0% of the time, Pallas kernels for 5%

profile of v4, /device:TPU:1, one launch (start us, length us, event | category | flops | bytes accessed | tf_op | source)
XLA Modules:
  0.0 43.8 jit_solution(3628052340682330540)
XLA Ops:
  0.6 4.7 %summary.1 = (bf16[16,24,128]{2,1,0:T(8,128)(2,1)S(1)}, f32[2,80,128]{2,1,0:T(8,128)S(1)}, f32[2048,128]{1,0:T(8,128)S(1)}, f32[16,128]{1,0:T(8,128)S(1)}) custom-call(s32[1]{0:T(128)} %bitcast.me_ref, bf16[1024,256]{1,0:T(8,128)(2,1)} %g_hbm.1, bf16[1024,256]{1,0:T(8,128)(2,1)} %x_hbm.1, f32[8,256]{1,0:T(8,128)} %bitcast.5, f32[8,256]{1,0:T(8,128)} %bitcast.6), custom_call_target="tpu_custom_call" | custom-call | tf_op jit(solution)/shard_map/summary/pallas_call | solution.py:311
  5.3 24.4 %all_to_all.10.got_ref = bf16[16,24,128]{2,1,0:T(8,128)(2,1)S(1)} all-to-all(bf16[16,24,128]{2,1,0:T(8,128)(2,1)S(1)} %get-tuple-element.9), channel_id=1, replica_groups={{10,0,1,3,2,4,12,5,7,13,15,6,14,8,9,11},{26,16,17,19,18,20,28,21,23,29,..., dimensions={0} | all-to-all | bytes 196608 | tf_op jit(solution)/shard_map/all_to_all | solution.py:297
  29.8 0.8 %join.1 = f32[32,2,128]{2,1,0:T(2,128)} custom-call(bf16[16,24,128]{2,1,0:T(8,128)(2,1)S(1)} %all_to_all.10.got_ref, f32[16,128]{1,0:T(8,128)S(1)} %get-tuple-element.12.own_ref), custom_call_target="tpu_custom_call" | custom-call | tf_op jit(solution)/shard_map/join/pallas_call | solution.py:339
  30.6 9.3 %all-to-all-start.1 = ((f32[32,2,128]{2,1,0:T(2,128)}), f32[32,2,128]{2,1,0:T(2,128)S(1)}, u32[]{:S(2)}, u32[]{:S(2)}) async-start(f32[32,2,128]{2,1,0:T(2,128)} %join.1), calls=%async_computation.1 | async-start | bytes 65536 | tf_op jit(solution)/shard_map/all_to_all | solution.py:297
  39.9 2.3 %input_gradient.1 = bf16[1024,256]{1,0:T(8,128)(2,1)} custom-call(s32[1]{0:T(128)} %bitcast.me_ref, bf16[16,24,128]{2,1,0:T(8,128)(2,1)S(1)} %all_to_all.10.got_ref, f32[2,80,128]{2,1,0:T(8,128)S(1)} %get-tuple-element.10.state_ref, f32[2048,128]{1,0:T(8,128)S(1)} %get-tuple-element.11.wide_ref), custom_call_target="tpu_custom_call" | custom-call | flops 8388608 | bytes 1048576 | tf_op jit(solution)/shard_map/input_gradient/pallas_call | solution.py:350
  42.2 0.9 %all-to-all-done.1.got_ref = f32[32,2,128]{2,1,0:T(2,128)S(1)} async-done(((f32[32,2,128]{2,1,0:T(2,128)}), f32[32,2,128]{2,1,0:T(2,128)S(1)}, u32[]{:S(2)}, u32[]{:S(2)}) %all-to-all-start.1) | async-done | bytes 32800 | tf_op jit(solution)/shard_map/all_to_all | solution.py:297
  43.1 0.7 %total.1 = (f32[8,16]{1,0:T(8,128)}, f32[8,16]{1,0:T(8,128)}) custom-call(f32[32,2,128]{2,1,0:T(2,128)S(1)} %all-to-all-done.1.got_ref), custom_call_target="tpu_custom_call" | custom-call | tf_op jit(solution)/shard_map/total/pallas_call | solution.py:367
Async XLA Ops:
  30.6 12.5 %all-to-all-start.1 = ((f32[32,2,128]{2,1,0:T(2,128)}), f32[32,2,128]{2,1,0:T(2,128)S(1)}, u32[]{:S(2)}, u32[]{:S(2)}) async-start(f32[32,2,128]{2,1,0:T(2,128)} %join.1), calls=%async_computation.1 | async-start | bytes 65536 | tf_op jit(solution)/shard_map/all_to_all | solution.py:297

commit v5 on v4

--- a/solution.py
+++ b/solution.py
@@ -12,13 +12,12 @@
 OWN = 16
 STEP = 4
 SOME = 2
-CTX_ORDER = [10, 0, 1, 3, 2, 4, 12, 5, 7, 13, 15, 6, 14, 8, 9, 11]
-DP_ORDER = [21, 22, 23, 24, 25, 26, 27, 28, 29, 30, 31, 0, 1, 2, 3, 4, 5, 6, 7, 8, 9, 10, 11, 12, 13, 14, 15, 16, 17, 18, 19, 20]
+CTX_ORDER = [10, 2, 3, 1, 0, 12, 13, 15, 14, 4, 5, 7, 6, 11, 9, 8]
+DP_ORDER = [23, 21, 22, 24, 25, 26, 27, 28, 29, 30, 31, 0, 1, 2, 3, 4, 5, 6, 7, 8, 9, 10, 11, 12, 13, 14, 15, 16, 17, 18, 19, 20]
 F32 = jnp.float32
 BF16 = jnp.bfloat16
 VMEM = pl.BlockSpec(memory_space=pltpu.VMEM)
 HBM = pl.BlockSpec(memory_space=pltpu.HBM)
-SMEM = pl.BlockSpec(memory_space=pltpu.SMEM)
 
 
 def interleave(src_ref, dst_ref, base):
@@ -38,7 +37,7 @@
 
 
 def summary_kernel(
-    seqlen, me_ref, g_hbm, x_hbm, lr_hbm, rs_hbm,
+    seqlen, g_hbm, x_hbm, lr_hbm, rs_hbm,
     send_ref, state_ref, wide_ref, own_ref,
     gb, xb, lr_ref, rs_ref, xs, acc, sems,
 ):
@@ -60,19 +59,16 @@
         [column(g_hbm, gb, half, sems.at[4 + half]), column(x_hbm, xb, half, sems.at[6 + half])]
         for half in range(halves)
     ]
-    for copy in large[0] + small:
+    for copy in large[0] + small + large[1]:
         copy.start()
+    for copy in small:
+        copy.wait()
 
     def scan(half):
         base = half * tokens
-        for copy, src, dst, at in zip(large[half], (gb, xb), (wide_ref, xs), (base, 0)):
-            copy.wait()
+        for i, (hbm, src, dst, at) in enumerate(((g_hbm, gb, wide_ref, base), (x_hbm, xb, xs, 0))):
+            column(hbm, src, half, sems.at[4 + 2 * i + half]).wait()
             interleave(src.at[half], dst, at)
-        if half == 0:
-            for copy in large[1]:
-                copy.start()
-            for copy in small:
-                copy.wait()
         rate = jnp.exp(lr_ref[half])
         zero = rate * 0.0
         for first in range(0, modes, SOME):
@@ -138,8 +134,7 @@
                     acc[half, j, (first + k) * SUBS : (first + k + 1) * SUBS, :] = values[j]
 
     both = range(halves)
-    for half in both:
-        scan(half)
+    pl.loop(0, halves)(scan)
 
     def of_run(j, c):
         return [acc[half, j, pl.ds(c, modes, stride=SUBS), :] for half in both]
@@ -183,7 +178,7 @@
             place = CTX_ORDER.index(half * (LANES // OWN) + d)
             send_ref[place, :, :] = jnp.concatenate([ahead, packed], axis=0).astype(BF16)
 
-    me = me_ref[0]
+    me = lax.axis_index("ctx")
     slots = LANES // OWN
     upper = me >= slots
     shift = jnp.where(me % slots == 0, 0, LANES - (me % slots) * OWN)
@@ -222,12 +217,12 @@
     send_ref[...] = jnp.broadcast_to(rows[None], send_ref.shape)
 
 
-def input_kernel(tokens, me_ref, got_ref, state_ref, wide_ref, out_hbm, os, ob, sems):
+def input_kernel(tokens, got_ref, state_ref, wide_ref, out_hbm, os, ob, sems):
     run = tokens // SUBS
     steps = run // STEP
     halves = state_ref.shape[0]
     modes = SUBS
-    me = me_ref[0]
+    me = lax.axis_index("ctx")
     rates = [state_ref[half, modes * SUBS : modes * SUBS + modes, :] for half in range(halves)]
     span = jnp.exp(-float(tokens) * jnp.concatenate(rates, axis=0))
     enter = jnp.zeros_like(span)
@@ -305,12 +300,11 @@
     modes = residues.shape[1]
     seqlen = tokens * n_context
     halves = chans // LANES
-    me = lax.axis_index("ctx").astype(jnp.int32).reshape(1)
     params = pltpu.CompilerParams(vmem_limit_bytes=24 * 1024 * 1024)
 
     send, state, wide, own = pl.pallas_call(
         functools.partial(summary_kernel, float(seqlen)),
-        in_specs=[SMEM, HBM, HBM, HBM, HBM],
+        in_specs=[HBM, HBM, HBM, HBM],
         out_specs=[VMEM, VMEM, VMEM, VMEM],
         out_shape=[
             jax.ShapeDtypeStruct((n_context, 3 * SUBS, LANES), BF16),
@@ -329,7 +323,7 @@
         ],
         compiler_params=params,
         name="summary",
-    )(me, *(
+    )(*(
         pltpu.with_memory_space_constraint(array, pltpu.HBM)
         for array in (grad_out, conv_input, log_rate.T, residues.T)
     ))
@@ -349,7 +343,7 @@
 
     grad_input = pl.pallas_call(
         functools.partial(input_kernel, tokens),
-        in_specs=[SMEM, VMEM, VMEM, VMEM],
+        in_specs=[VMEM, VMEM, VMEM],
         out_specs=HBM,
         out_shape=jax.ShapeDtypeStruct((tokens, chans), BF16),
         scratch_shapes=[
@@ -362,7 +356,7 @@
             flops=4 * tokens * chans * modes, bytes_accessed=4 * tokens * chans, transcendentals=0
         ),
         name="input_gradient",
-    )(me, got, state, wide)
+    )(got, state, wide)
 
     grad_residue, grad_lograte = pl.pallas_call(
         total_kernel,

time: 44 us -> 43.6 us (level)
  waiting for transfers between devices: 0.94 us -> 0.04 us
  blocking collectives: 24.4 us -> 25 us
    all_to_all x1, waiting for transfers between devices: 0.94 us -> 0.04 us  [exchange(): lax.all_to_all(blocks, axis, split_axis=0, concat_axis=0, axis_index_grou...]
    all_to_all x1, blocking collectives: 24.4 us -> 25 us  [exchange(): lax.all_to_all(blocks, axis, split_axis=0, concat_axis=0, axis_index_grou...]
  transfers between devices with their start and end apart: 1 -> 1, of which waited for: 1 -> 0; matrix products, arithmetic and copies ran while one was open for 0% -> 0% of each run, Pallas kernels for 5% -> 5%
where the time goes in v5:
time: 43.6 us; the launch traced here: 43.4 us
  blocking collectives  25 us (57%)
  starting transfers between devices  9.23 us (21%)
  Pallas kernels  8.45 us (19%)
  between operations  0.66 us (2%)
    all_to_all x1, blocking collectives, exchange(): lax.all_to_all(blocks, axis, split_axis=0, concat_axis=0, axis_index_grou...  25 us
    all_to_all x1, starting transfers between devices, exchange(): lax.all_to_all(blocks, axis, split_axis=0, concat_axis=0, axis_index_grou...  9.23 us
    pallas_call x1, Pallas kernels, on_device(): pl.pallas_call(functools.partial(summary_kernel, float(seqlen)), in_specs...  4.66 us
    pallas_call x1, Pallas kernels, on_device(): pl.pallas_call(functools.partial(input_kernel, tokens), in_specs=[VMEM, V...  2.27 us
  transfers between devices with their start and end apart: 1, of which 0 were waited for; matrix products, arithmetic and copies ran while one was open for 0% of the time, Pallas kernels for 5%

profile of v5, /device:TPU:1, one launch (start us, length us, event | category | flops | bytes accessed | tf_op | source)
XLA Modules:
  0.0 43.4 jit_solution(10132175506728318168)
XLA Ops:
  0.6 4.7 %summary.1 = (bf16[16,24,128]{2,1,0:T(8,128)(2,1)S(1)}, f32[2,80,128]{2,1,0:T(8,128)S(1)}, f32[2048,128]{1,0:T(8,128)S(1)}, f32[16,128]{1,0:T(8,128)S(1)}) custom-call(bf16[1024,256]{1,0:T(8,128)(2,1)} %g_hbm.1, bf16[1024,256]{1,0:T(8,128)(2,1)} %x_hbm.1, f32[8,256]{1,0:T(8,128)} %bitcast.4, f32[8,256]{1,0:T(8,128)} %bitcast.5), custom_call_target="tpu_custom_call" | custom-call | tf_op jit(solution)/shard_map/summary/pallas_call | solution.py:305
  5.3 25.0 %all_to_all.10.got_ref = bf16[16,24,128]{2,1,0:T(8,128)(2,1)S(1)} all-to-all(bf16[16,24,128]{2,1,0:T(8,128)(2,1)S(1)} %get-tuple-element.9), channel_id=1, replica_groups={{10,2,3,1,0,12,13,15,14,4,5,7,6,11,9,8},{26,18,19,17,16,28,29,31,30,20,..., dimensions={0} | all-to-all | bytes 196608 | tf_op jit(solution)/shard_map/all_to_all | solution.py:292
  30.3 0.8 %join.1 = f32[32,2,128]{2,1,0:T(2,128)} custom-call(bf16[16,24,128]{2,1,0:T(8,128)(2,1)S(1)} %all_to_all.10.got_ref, f32[16,128]{1,0:T(8,128)S(1)} %get-tuple-element.12.own_ref), custom_call_target="tpu_custom_call" | custom-call | tf_op jit(solution)/shard_map/join/pallas_call | solution.py:333
  31.1 9.2 %all-to-all-start.1 = ((f32[32,2,128]{2,1,0:T(2,128)}), f32[32,2,128]{2,1,0:T(2,128)S(1)}, u32[]{:S(2)}, u32[]{:S(2)}) async-start(f32[32,2,128]{2,1,0:T(2,128)} %join.1), calls=%async_computation.1 | async-start | bytes 65536 | tf_op jit(solution)/shard_map/all_to_all | solution.py:292
  40.3 2.3 %input_gradient.1 = bf16[1024,256]{1,0:T(8,128)(2,1)} custom-call(bf16[16,24,128]{2,1,0:T(8,128)(2,1)S(1)} %all_to_all.10.got_ref, f32[2,80,128]{2,1,0:T(8,128)S(1)} %get-tuple-element.10.state_ref, f32[2048,128]{1,0:T(8,128)S(1)} %get-tuple-element.11.wide_ref), custom_call_target="tpu_custom_call" | custom-call | flops 8388608 | bytes 1048576 | tf_op jit(solution)/shard_map/input_gradient/pallas_call | solution.py:344
  42.6 0.0 all-to-all-done.1.got_ref
  42.7 0.7 %total.1 = (f32[8,16]{1,0:T(8,128)}, f32[8,16]{1,0:T(8,128)}) custom-call(f32[32,2,128]{2,1,0:T(2,128)S(1)} %all-to-all-done.1.got_ref), custom_call_target="tpu_custom_call" | custom-call | tf_op jit(solution)/shard_map/total/pallas_call | solution.py:361
Async XLA Ops:
  31.1 11.6 %all-to-all-start.1 = ((f32[32,2,128]{2,1,0:T(2,128)}), f32[32,2,128]{2,1,0:T(2,128)S(1)}, u32[]{:S(2)}, u32[]{:S(2)}) async-start(f32[32,2,128]{2,1,0:T(2,128)} %join.1), calls=%async_computation.1 | async-start | bytes 65536 | tf_op jit(solution)/shard_map/all_to_all | solution.py:292

commit v6 on v5

--- a/solution.py
+++ b/solution.py
@@ -23,7 +23,7 @@
 def interleave(src_ref, dst_ref, base):
     run = src_ref.shape[0] // SUBS
 
-    @pl.loop(0, run // 16)
+    @pl.loop(0, run // 16, unroll=8)
     def _(i):
         for c in range(SUBS):
             rows = src_ref[pl.ds(pl.multiple_of(c * run + i * 16, 16), 16), :]
@@ -63,6 +63,16 @@
         copy.start()
     for copy in small:
         copy.wait()
+
+    me = lax.axis_index("ctx")
+    slots = LANES // OWN
+    upper = me >= slots
+    shift = jnp.where(me % slots == 0, 0, LANES - (me % slots) * OWN)
+    rate = jnp.exp(pltpu.roll(jnp.where(upper, lr_ref[1], lr_ref[0]), shift, 1))
+    resid = pltpu.roll(jnp.where(upper, rs_ref[1], rs_ref[0]), shift, 1)
+    own_ref[0:SUBS, :] = jnp.exp(-float(tokens) * rate)
+    own_ref[SUBS : 2 * SUBS, :] = -rate * resid * (1.0 / seqlen)
+
 
     def scan(half):
         base = half * tokens
@@ -178,15 +188,6 @@
             place = CTX_ORDER.index(half * (LANES // OWN) + d)
             send_ref[place, :, :] = jnp.concatenate([ahead, packed], axis=0).astype(BF16)
 
-    me = lax.axis_index("ctx")
-    slots = LANES // OWN
-    upper = me >= slots
-    shift = jnp.where(me % slots == 0, 0, LANES - (me % slots) * OWN)
-    rate = jnp.exp(pltpu.roll(jnp.where(upper, lr_ref[1], lr_ref[0]), shift, 1))
-    resid = pltpu.roll(jnp.where(upper, rs_ref[1], rs_ref[0]), shift, 1)
-    own_ref[0:SUBS, :] = jnp.exp(-float(tokens) * rate)
-    own_ref[SUBS : 2 * SUBS, :] = -rate * resid * (1.0 / seqlen)
-
 
 def join_kernel(seqlen, tokens, got_ref, own_ref, send_ref):
     blocks = got_ref.shape[0]
@@ -262,9 +263,9 @@
             os[pl.ds(pl.multiple_of(b * size, size), size), :] = jnp.concatenate(sums, axis=0)
             return carry
 
-        lax.fori_loop(0, steps, step, tuple(start), unroll=2)
-
-        @pl.loop(0, run // 16)
+        lax.fori_loop(0, steps, step, tuple(start), unroll=4)
+
+        @pl.loop(0, run // 16, unroll=8)
         def _(i):
             for c in range(SUBS):
                 rows = os[pl.ds(i * (16 * SUBS) + c, 16, stride=SUBS), :]

time: 43.6 us -> 43.4 us (level)
  transfers between devices with their start and end apart: 1 -> 1, of which waited for: 0 -> 1; matrix products, arithmetic and copies ran while one was open for 0% -> 0% of each run, Pallas kernels for 5% -> 5%
where the time goes in v6:
time: 43.4 us; the launch traced here: 43.2 us
  blocking collectives  25 us (58%)
  starting transfers between devices  9.23 us (21%)
  Pallas kernels  8.08 us (19%)
  between operations  0.66 us (2%)
    all_to_all x1, blocking collectives, exchange(): lax.all_to_all(blocks, axis, split_axis=0, concat_axis=0, axis_index_grou...  25 us
    all_to_all x1, starting transfers between devices, exchange(): lax.all_to_all(blocks, axis, split_axis=0, concat_axis=0, axis_index_grou...  9.23 us
    pallas_call x1, Pallas kernels, on_device(): pl.pallas_call(functools.partial(summary_kernel, float(seqlen)), in_specs...  4.45 us
    pallas_call x1, Pallas kernels, on_device(): pl.pallas_call(functools.partial(input_kernel, tokens), in_specs=[VMEM, V...  2.11 us
  transfers between devices with their start and end apart: 1, of which 1 were waited for; matrix products, arithmetic and copies ran while one was open for 0% of the time, Pallas kernels for 5%

profile of v6, /device:TPU:1, one launch (start us, length us, event | category | flops | bytes accessed | tf_op | source)
XLA Modules:
  0.0 43.2 jit_solution(12217813278353641366)
XLA Ops:
  0.6 4.5 %summary.1 = (bf16[16,24,128]{2,1,0:T(8,128)(2,1)S(1)}, f32[2,80,128]{2,1,0:T(8,128)S(1)}, f32[2048,128]{1,0:T(8,128)S(1)}, f32[16,128]{1,0:T(8,128)S(1)}) custom-call(bf16[1024,256]{1,0:T(8,128)(2,1)} %g_hbm.1, bf16[1024,256]{1,0:T(8,128)(2,1)} %x_hbm.1, f32[8,256]{1,0:T(8,128)} %bitcast.4, f32[8,256]{1,0:T(8,128)} %bitcast.5), custom_call_target="tpu_custom_call" | custom-call | tf_op jit(solution)/shard_map/summary/pallas_call | solution.py:306
  5.1 25.0 %all_to_all.10.got_ref = bf16[16,24,128]{2,1,0:T(8,128)(2,1)S(1)} all-to-all(bf16[16,24,128]{2,1,0:T(8,128)(2,1)S(1)} %get-tuple-element.9), channel_id=1, replica_groups={{10,2,3,1,0,12,13,15,14,4,5,7,6,11,9,8},{26,18,19,17,16,28,29,31,30,20,..., dimensions={0} | all-to-all | bytes 196608 | tf_op jit(solution)/shard_map/all_to_all | solution.py:293
  30.1 0.8 %join.1 = f32[32,2,128]{2,1,0:T(2,128)} custom-call(bf16[16,24,128]{2,1,0:T(8,128)(2,1)S(1)} %all_to_all.10.got_ref, f32[16,128]{1,0:T(8,128)S(1)} %get-tuple-element.12.own_ref), custom_call_target="tpu_custom_call" | custom-call | tf_op jit(solution)/shard_map/join/pallas_call | solution.py:334
  30.9 9.2 %all-to-all-start.1 = ((f32[32,2,128]{2,1,0:T(2,128)}), f32[32,2,128]{2,1,0:T(2,128)S(1)}, u32[]{:S(2)}, u32[]{:S(2)}) async-start(f32[32,2,128]{2,1,0:T(2,128)} %join.1), calls=%async_computation.1 | async-start | bytes 65536 | tf_op jit(solution)/shard_map/all_to_all | solution.py:293
  40.1 2.1 %input_gradient.1 = bf16[1024,256]{1,0:T(8,128)(2,1)} custom-call(bf16[16,24,128]{2,1,0:T(8,128)(2,1)S(1)} %all_to_all.10.got_ref, f32[2,80,128]{2,1,0:T(8,128)S(1)} %get-tuple-element.10.state_ref, f32[2048,128]{1,0:T(8,128)S(1)} %get-tuple-element.11.wide_ref), custom_call_target="tpu_custom_call" | custom-call | flops 8388608 | bytes 1048576 | tf_op jit(solution)/shard_map/input_gradient/pallas_call | solution.py:345
  42.2 0.2 all-to-all-done.1.got_ref
  42.4 0.7 %total.1 = (f32[8,16]{1,0:T(8,128)}, f32[8,16]{1,0:T(8,128)}) custom-call(f32[32,2,128]{2,1,0:T(2,128)S(1)} %all-to-all-done.1.got_ref), custom_call_target="tpu_custom_call" | custom-call | tf_op jit(solution)/shard_map/total/pallas_call | solution.py:362
Async XLA Ops:
  30.9 11.6 %all-to-all-start.1 = ((f32[32,2,128]{2,1,0:T(2,128)}), f32[32,2,128]{2,1,0:T(2,128)S(1)}, u32[]{:S(2)}, u32[]{:S(2)}) async-start(f32[32,2,128]{2,1,0:T(2,128)} %join.1), calls=%async_computation.1 | async-start | bytes 65536 | tf_op jit(solution)/shard_map/all_to_all | solution.py:293

commit v7 on v6

--- a/solution.py
+++ b/solution.py
@@ -189,6 +189,12 @@
             send_ref[place, :, :] = jnp.concatenate([ahead, packed], axis=0).astype(BF16)
 
 
+def add_up(terms):
+    while len(terms) > 1:
+        terms = [a + b for a, b in zip(terms[::2], terms[1::2])] + terms[len(terms) & ~1 :]
+    return terms[0]
+
+
 def join_kernel(seqlen, tokens, got_ref, own_ref, send_ref):
     blocks = got_ref.shape[0]
 
@@ -196,16 +202,18 @@
         return pltpu.roll(tile, LANES - OWN * j, 1)
 
     span = own_ref[0:SUBS, :]
-    w = q = res = lag = every = jnp.zeros((SUBS, LANES), F32)
+    w = q = jnp.zeros((SUBS, LANES), F32)
+    tiles, res, lag = [], [], []
     for k in range(blocks - 1, -1, -1):
         tile = got_ref[CTX_ORDER.index(k), :, :].astype(F32)[2 * SUBS : 3 * SUBS]
-        every = every + tile
         near = slot(tile, 2)
-        res = res + near * w
-        lag = lag + near * q + slot(tile, 3) * w
+        tiles.append(tile)
+        res.append(near * w)
+        lag.append(near * q + slot(tile, 3) * w)
         z = span * w
-        q = slot(tile, 1) + span * q + float(tokens) * z
+        q = (slot(tile, 1) + float(tokens) * z) + span * q
         w = tile + z
+    every, res, lag = add_up(tiles), add_up(res), add_up(lag)
     res = (res + (slot(every, 4) + slot(every, 6))) * (1.0 / seqlen)
     lag = (lag + (slot(every, 5) + slot(every, 7))) * own_ref[SUBS : 2 * SUBS, :]
     lane = lax.broadcasted_iota(jnp.int32, (SUBS, LANES), 1)
@@ -256,9 +264,7 @@
             for j in range(STEP - 1, -1, -1):
                 carry = tuple(a * w + values[j] for a, w in zip(decay, carry))
                 terms = [r * w for r, w in zip(resid, carry)]
-                while len(terms) > 1:
-                    terms = [a + b for a, b in zip(terms[::2], terms[1::2])]
-                sums[j] = terms[0]
+                sums[j] = add_up(terms)
             size = STEP * SUBS
             os[pl.ds(pl.multiple_of(b * size, size), size), :] = jnp.concatenate(sums, axis=0)
             return carry
@@ -277,9 +283,7 @@
 
 
 def total_kernel(got_ref, res_ref, lag_ref):
-    total = got_ref[0, :, :]
-    for k in range(1, got_ref.shape[0]):
-        total = total + got_ref[k, :, :]
+    total = add_up([got_ref[k, :, :] for k in range(got_ref.shape[0])])
     mode = lax.broadcasted_iota(jnp.int32, (SUBS, LANES), 0)
     for j, out in enumerate((res_ref, lag_ref)):
         row = jnp.broadcast_to(total[j : j + 1], (SUBS, LANES))

time: 43.4 us -> 43.3 us (level)
  no operation moved by 1% of the time
where the time goes in v7:
time: 43.3 us; the launch traced here: 43.1 us
  blocking collectives  25 us (58%)
  starting transfers between devices  9.23 us (21%)
  Pallas kernels  8.05 us (19%)
  between operations  0.66 us (2%)
    all_to_all x1, blocking collectives, exchange(): lax.all_to_all(blocks, axis, split_axis=0, concat_axis=0, axis_index_grou...  25 us
    all_to_all x1, starting transfers between devices, exchange(): lax.all_to_all(blocks, axis, split_axis=0, concat_axis=0, axis_index_grou...  9.23 us
    pallas_call x1, Pallas kernels, on_device(): pl.pallas_call(functools.partial(summary_kernel, float(seqlen)), in_specs...  4.45 us
    pallas_call x1, Pallas kernels, on_device(): pl.pallas_call(functools.partial(input_kernel, tokens), in_specs=[VMEM, V...  2.11 us
  transfers between devices with their start and end apart: 1, of which 1 were waited for; matrix products, arithmetic and copies ran while one was open for 0% of the time, Pallas kernels for 5%

profile of v7, /device:TPU:1, one launch (start us, length us, event | category | flops | bytes accessed | tf_op | source)
XLA Modules:
  0.0 43.1 jit_solution(686086926612420213)
XLA Ops:
  0.6 4.5 %summary.1 = (bf16[16,24,128]{2,1,0:T(8,128)(2,1)S(1)}, f32[2,80,128]{2,1,0:T(8,128)S(1)}, f32[2048,128]{1,0:T(8,128)S(1)}, f32[16,128]{1,0:T(8,128)S(1)}) custom-call(bf16[1024,256]{1,0:T(8,128)(2,1)} %g_hbm.1, bf16[1024,256]{1,0:T(8,128)(2,1)} %x_hbm.1, f32[8,256]{1,0:T(8,128)} %bitcast.4, f32[8,256]{1,0:T(8,128)} %bitcast.5), custom_call_target="tpu_custom_call" | custom-call | tf_op jit(solution)/shard_map/summary/pallas_call | solution.py:310
  5.1 25.0 %all_to_all.10.got_ref = bf16[16,24,128]{2,1,0:T(8,128)(2,1)S(1)} all-to-all(bf16[16,24,128]{2,1,0:T(8,128)(2,1)S(1)} %get-tuple-element.9), channel_id=1, replica_groups={{10,2,3,1,0,12,13,15,14,4,5,7,6,11,9,8},{26,18,19,17,16,28,29,31,30,20,..., dimensions={0} | all-to-all | bytes 196608 | tf_op jit(solution)/shard_map/all_to_all | solution.py:297
  30.1 0.8 %join.1 = f32[32,2,128]{2,1,0:T(2,128)} custom-call(bf16[16,24,128]{2,1,0:T(8,128)(2,1)S(1)} %all_to_all.10.got_ref, f32[16,128]{1,0:T(8,128)S(1)} %get-tuple-element.12.own_ref), custom_call_target="tpu_custom_call" | custom-call | tf_op jit(solution)/shard_map/join/pallas_call | solution.py:338
  30.9 9.2 %all-to-all-start.1 = ((f32[32,2,128]{2,1,0:T(2,128)}), f32[32,2,128]{2,1,0:T(2,128)S(1)}, u32[]{:S(2)}, u32[]{:S(2)}) async-start(f32[32,2,128]{2,1,0:T(2,128)} %join.1), calls=%async_computation.1 | async-start | bytes 65536 | tf_op jit(solution)/shard_map/all_to_all | solution.py:297
  40.1 2.1 %input_gradient.1 = bf16[1024,256]{1,0:T(8,128)(2,1)} custom-call(bf16[16,24,128]{2,1,0:T(8,128)(2,1)S(1)} %all_to_all.10.got_ref, f32[2,80,128]{2,1,0:T(8,128)S(1)} %get-tuple-element.10.state_ref, f32[2048,128]{1,0:T(8,128)S(1)} %get-tuple-element.11.wide_ref), custom_call_target="tpu_custom_call" | custom-call | flops 8388608 | bytes 1048576 | tf_op jit(solution)/shard_map/input_gradient/pallas_call | solution.py:349
  42.2 0.2 all-to-all-done.1.got_ref
  42.4 0.7 %total.1 = (f32[8,16]{1,0:T(8,128)}, f32[8,16]{1,0:T(8,128)}) custom-call(f32[32,2,128]{2,1,0:T(2,128)S(1)} %all-to-all-done.1.got_ref), custom_call_target="tpu_custom_call" | custom-call | tf_op jit(solution)/shard_map/total/pallas_call | solution.py:366
Async XLA Ops:
  30.9 11.6 %all-to-all-start.1 = ((f32[32,2,128]{2,1,0:T(2,128)}), f32[32,2,128]{2,1,0:T(2,128)S(1)}, u32[]{:S(2)}, u32[]{:S(2)}) async-start(f32[32,2,128]{2,1,0:T(2,128)} %join.1), calls=%async_computation.1 | async-start | bytes 65536 | tf_op jit(solution)/shard_map/all_to_all | solution.py:297

commit v8 on v7

--- a/solution.py
+++ b/solution.py
@@ -81,11 +81,12 @@
             interleave(src.at[half], dst, at)
         rate = jnp.exp(lr_ref[half])
         zero = rate * 0.0
+        once, four = jnp.exp(-rate), jnp.exp(-float(STEP) * rate)
         for first in range(0, modes, SOME):
-            rows = [jnp.broadcast_to(rate[m : m + 1], (SUBS, LANES)) for m in range(first, first + SOME)]
-            decay = [jnp.exp(-r) for r in rows]
+            group = range(first, first + SOME)
+            decay = [jnp.broadcast_to(once[m : m + 1], (SUBS, LANES)) for m in group]
             part = [a * (1.0 / STEP) for a in decay]
-            leap = [jnp.exp(-float(STEP) * r) for r in rows]
+            leap = [jnp.broadcast_to(four[m : m + 1], (SUBS, LANES)) for m in group]
 
             def step(i, carry):
                 b = steps - 1 - i
@@ -180,11 +181,17 @@
             w[half], q[half], near[half], far[half],
             res_high, lag_high, res[half] - res_high, lag[half] - lag_high,
         )
-        for d in range(LANES // OWN):
-            packed = parts[d]
-            for j, part in enumerate(parts):
-                if j != d:
-                    packed = jnp.where(slot == j, pltpu.roll(part, ((j - d) * OWN) % LANES, 1), packed)
+        slots = LANES // OWN
+        turned = []
+        for r in range(slots):
+            mixed = parts[r]
+            for p in range(1, slots):
+                mixed = jnp.where(slot == p, parts[(p + r) % slots], mixed)
+            turned.append(pltpu.roll(mixed, r * OWN, 1) if r else mixed)
+        for d in range(slots):
+            packed = turned[-d % slots]
+            for j in range(1, slots):
+                packed = jnp.where(slot == j, turned[(j - d) % slots], packed)
             place = CTX_ORDER.index(half * (LANES // OWN) + d)
             send_ref[place, :, :] = jnp.concatenate([ahead, packed], axis=0).astype(BF16)
 

time: 43.3 us -> 43.3 us (level)
  no operation moved by 1% of the time
where the time goes in v8:
time: 43.3 us; the launch traced here: 43.1 us
  blocking collectives  25 us (58%)
  starting transfers between devices  9.23 us (21%)
  Pallas kernels  8.02 us (19%)
  between operations  0.66 us (2%)
    all_to_all x1, blocking collectives, exchange(): lax.all_to_all(blocks, axis, split_axis=0, concat_axis=0, axis_index_grou...  25 us
    all_to_all x1, starting transfers between devices, exchange(): lax.all_to_all(blocks, axis, split_axis=0, concat_axis=0, axis_index_grou...  9.23 us
    pallas_call x1, Pallas kernels, on_device(): pl.pallas_call(functools.partial(summary_kernel, float(seqlen)), in_specs...  4.43 us
    pallas_call x1, Pallas kernels, on_device(): pl.pallas_call(functools.partial(input_kernel, tokens), in_specs=[VMEM, V...  2.11 us
  transfers between devices with their start and end apart: 1, of which 1 were waited for; matrix products, arithmetic and copies ran while one was open for 0% of the time, Pallas kernels for 5%

profile of v8, /device:TPU:1, one launch (start us, length us, event | category | flops | bytes accessed | tf_op | source)
XLA Modules:
  0.0 43.1 jit_solution(15114930524951922225)
XLA Ops:
  0.6 4.4 %summary.1 = (bf16[16,24,128]{2,1,0:T(8,128)(2,1)S(1)}, f32[2,80,128]{2,1,0:T(8,128)S(1)}, f32[2048,128]{1,0:T(8,128)S(1)}, f32[16,128]{1,0:T(8,128)S(1)}) custom-call(bf16[1024,256]{1,0:T(8,128)(2,1)} %g_hbm.1, bf16[1024,256]{1,0:T(8,128)(2,1)} %x_hbm.1, f32[8,256]{1,0:T(8,128)} %bitcast.4, f32[8,256]{1,0:T(8,128)} %bitcast.5), custom_call_target="tpu_custom_call" | custom-call | tf_op jit(solution)/shard_map/summary/pallas_call | solution.py:317
  5.1 25.0 %all_to_all.10.got_ref = bf16[16,24,128]{2,1,0:T(8,128)(2,1)S(1)} all-to-all(bf16[16,24,128]{2,1,0:T(8,128)(2,1)S(1)} %get-tuple-element.9), channel_id=1, replica_groups={{10,2,3,1,0,12,13,15,14,4,5,7,6,11,9,8},{26,18,19,17,16,28,29,31,30,20,..., dimensions={0} | all-to-all | bytes 196608 | tf_op jit(solution)/shard_map/all_to_all | solution.py:304
  30.1 0.8 %join.1 = f32[32,2,128]{2,1,0:T(2,128)} custom-call(bf16[16,24,128]{2,1,0:T(8,128)(2,1)S(1)} %all_to_all.10.got_ref, f32[16,128]{1,0:T(8,128)S(1)} %get-tuple-element.12.own_ref), custom_call_target="tpu_custom_call" | custom-call | tf_op jit(solution)/shard_map/join/pallas_call | solution.py:345
  30.9 9.2 %all-to-all-start.1 = ((f32[32,2,128]{2,1,0:T(2,128)}), f32[32,2,128]{2,1,0:T(2,128)S(1)}, u32[]{:S(2)}, u32[]{:S(2)}) async-start(f32[32,2,128]{2,1,0:T(2,128)} %join.1), calls=%async_computation.1 | async-start | bytes 65536 | tf_op jit(solution)/shard_map/all_to_all | solution.py:304
  40.1 2.1 %input_gradient.1 = bf16[1024,256]{1,0:T(8,128)(2,1)} custom-call(bf16[16,24,128]{2,1,0:T(8,128)(2,1)S(1)} %all_to_all.10.got_ref, f32[2,80,128]{2,1,0:T(8,128)S(1)} %get-tuple-element.10.state_ref, f32[2048,128]{1,0:T(8,128)S(1)} %get-tuple-element.11.wide_ref), custom_call_target="tpu_custom_call" | custom-call | flops 8388608 | bytes 1048576 | tf_op jit(solution)/shard_map/input_gradient/pallas_call | solution.py:356
  42.2 0.2 all-to-all-done.1.got_ref
  42.4 0.7 %total.1 = (f32[8,16]{1,0:T(8,128)}, f32[8,16]{1,0:T(8,128)}) custom-call(f32[32,2,128]{2,1,0:T(2,128)S(1)} %all-to-all-done.1.got_ref), custom_call_target="tpu_custom_call" | custom-call | tf_op jit(solution)/shard_map/total/pallas_call | solution.py:373
Async XLA Ops:
  30.9 11.6 %all-to-all-start.1 = ((f32[32,2,128]{2,1,0:T(2,128)}), f32[32,2,128]{2,1,0:T(2,128)S(1)}, u32[]{:S(2)}, u32[]{:S(2)}) async-start(f32[32,2,128]{2,1,0:T(2,128)} %join.1), calls=%async_computation.1 | async-start | bytes 65536 | tf_op jit(solution)/shard_map/all_to_all | solution.py:304
